TPU v7x, 128 devices: a whole 4x4x4 slice. The times are simulated.
128 devices in a mesh: grp: 16 (over z, x), lane: 8 (over y, core).
Axes of the slice: x: 4, y: 4, z: 4, core: 2. Of those that a mesh axis runs over, the one named last changes fastest.
Arguments:
- coords: float32 [3, 786432], P(None, ('grp', 'lane')), may hold values from 0 to 1, as said below
- charges: float32 [64, 786432], P(None, ('grp', 'lane')), may hold values from -0.9 to 0.9
- basis: float32 [256, 196608], P(None, ('grp', 'lane')), may hold values from -0.75 to 0.75
- transfer1: float32 [64, 196608], P(None, ('grp', 'lane')), may hold values from -0.375 to 0.375
- transfer2: float32 [64, 49152], P(None, ('grp', 'lane')), may hold values from -0.75 to 0.75
- coupling0: float32 [8, 64, 196608], P(None, None, ('grp', 'lane')), may hold values from -0.25 to 0.25
- coupling1: float32 [4, 64, 49152], P(None, None, ('grp', 'lane')), may hold values from -0.375 to 0.375
- coupling2: float32 [4, 64, 1024], P(None, None, 'grp'), may hold values from -0.375 to 0.375
- near_list: int32 [3072, 9], P(('grp', 'lane')), may hold values from 0 to 3071, as said below
- near_count: int32 [3072], P(('grp', 'lane')), may hold values from 2 to 9
- far0_list: int32 [3072, 8], P(('grp', 'lane')), may hold values from 0 to 3071, as said below
- far1_list: int32 [768, 4], P(('grp', 'lane')), may hold values from 0 to 767, as said below
- far2_list: int32 [16, 4], replicated, may hold values from 0 to 15, as said below
Outputs:
- potential: float32 [64, 786432], P(None, ('grp', 'lane'))
Inputs may be any that keep to these rules, and one draw needn't show every extreme that they name: `coords`: the points lie on a torus inside the unit cube; the points of one leaf form a small patch of it, and leaves close in order are close on the surface. `near_list`: row l starts with l itself; its other entries are distinct leaves 1 to 24 positions away from l, cyclically over 3072, and none of them stands in row l of far0_list. `far0_list`: distinct leaves 1 to 24 positions away from l, cyclically over 3072. `far1_list`: distinct middle clusters 1 to 6 positions away from m, cyclically over 768. `far2_list`: distinct top clusters other than g.
All inputs are finite; a program needn't handle non-finite values.
Results may differ from a plain program's by a relative error of at most 0.0003.
Values sent between devices are 32-bit elements; how exact they have to be, the bound alone decides.
A program may use at most 128 MiB of HBM per device.

v0:
```python
import math

import jax
import jax.numpy as jnp
from jax import lax
from jax.experimental import pallas as pl
from jax.experimental.pallas import tpu as pltpu
from jax.sharding import PartitionSpec as P

AXES = ("grp", "lane")
LANES = 8
DEVS = 128
LEAF = 24
MID = 6
PTS = 256
RANK = 64
NEAR = 9
FAR0 = 8
FAR1 = 4
FAR2 = 4
UNROLL = 12
LIST = 256
inv_four_pi = 1.0 / (4.0 * math.pi)
smooth_sq = 5e-05
bf16 = jnp.bfloat16
f32 = jnp.float32
NT = (((1,), (1,)), ((), ()))


def dot(a, b, dims=(((1,), (0,)), ((), ()))):
    return lax.dot_general(a, b, dims, preferred_element_type=f32)


def split(a):
    high = a.astype(bf16)
    return high, (a - high.astype(f32)).astype(bf16)


def lanes_low(shape):
    return lax.broadcasted_iota(jnp.int32, shape, len(shape) - 1) < RANK


def swap_halves(a):
    return pltpu.roll(a, RANK, 1)


def halves(tile):
    low = lanes_low(tile.shape)
    return jnp.where(low, tile, 0.0), jnp.where(low, 0.0, tile)


def place_of():
    return lax.axis_index("grp") * LANES + lax.axis_index("lane")


def relative(entry, place, width):
    rel = lax.rem(entry - place * width + (DEVS + 1) * width, DEVS * width)
    cat = rel // width
    index = rel - cat * width
    other = jnp.where(lax.rem(place, 2) == 0, 2, 0)
    block = jnp.where(cat == 1, 0, jnp.where(cat == other, 1, 2))
    return block, index


def stacked_split(rows_a, rows_b):
    ah, al = split(rows_a)
    bh, bl = split(rows_b)
    return jnp.concatenate([ah, bh, al, bl], axis=0)


def wide_split(a):
    h, l = split(a)
    return jnp.concatenate([h, l], axis=1)


def fold(out):
    s = out[:, :128] + out[:, 128:]
    return s[0:64] + s[128:192], s[64:128] + s[192:256]


def transposed(rows_a, rows_b, weights):
    lhs = stacked_split(rows_a, rows_b)
    wh, wl = split(weights)
    r = dot(lhs, wh, NT)
    r2 = dot(lhs[:128], wl, NT)
    return r[0:64] + r[128:192] + r2[0:64], r[64:128] + r[192:256] + r2[64:128]


def up_kernel(near_ref, count_ref, coords_ref, x_ref, basis_ref, t1_ref, t2_ref, pack_ref, top_ref, list_ref, n_ref):
    place = place_of()
    tiles = []
    for t in range(LEAF // 2):
        xa = x_ref[:, t * 512:t * 512 + 256]
        xb = x_ref[:, t * 512 + 256:t * 512 + 512]
        ra, rb = fold(dot(stacked_split(xa, xb), wide_split(basis_ref[:, t * 128:t * 128 + 128])))
        q = jnp.where(lanes_low(ra.shape), ra, rb)
        pack_ref[t] = q
        tiles.append(q)
    mids = []
    parts = []
    for m in range(MID):
        a0, b0 = halves(tiles[2 * m])
        a1, b1 = halves(tiles[2 * m + 1])
        e0 = t1_ref[:, m * 256:m * 256 + 128]
        e1 = t1_ref[:, m * 256 + 128:m * 256 + 256]
        lhs = stacked_split(jnp.concatenate([a0, a1], axis=1), jnp.concatenate([b0, b1], axis=1))
        parts.append(fold(dot(lhs, wide_split(jnp.concatenate([e0, e0, e1, e1], axis=0)))))
    for t in range(MID // 2):
        (top0, bot0), (top1, bot1) = parts[2 * t], parts[2 * t + 1]
        low = lanes_low(top0.shape)
        mid = jnp.where(low, top0, bot1) + swap_halves(jnp.where(low, top1, bot0))
        pack_ref[LEAF // 2 + t] = mid
        mids.append(mid)
    both = [halves(m) for m in mids]
    weights = [t2_ref[:, t * 128:t * 128 + 128] for t in range(MID // 2)]
    lhs = stacked_split(
        jnp.concatenate([b[0] for b in both], axis=1), jnp.concatenate([b[1] for b in both], axis=1)
    )
    top, bot = fold(dot(lhs, wide_split(jnp.concatenate([w for w in weights for _ in range(2)], axis=0))))
    s = jnp.where(lanes_low(top.shape), top, bot)
    s = s + swap_halves(s)
    top_ref[...] = jnp.where(lanes_low((32, 128)), s[:32], s[32:])
    for i in range(2 * LEAF):
        for c in range(3):
            pack_ref[15 + c, i:i + 1, :] = coords_ref[c:c + 1, i * 128:i * 128 + 128]
    zero = jnp.zeros((16, 128), f32)
    for c in range(3):
        pack_ref[15 + c, 48:64, :] = zero

    def leaf_step(leaf, at):
        live = count_ref[leaf]
        for k in range(NEAR):
            block, index = relative(near_ref[leaf, k], place, LEAF)
            one = jnp.where(live > k, 1, 0)
            pos = jnp.where(block == 0, at[0], jnp.where(block == 1, at[1], at[2]))
            list_ref[2 * block, pos] = leaf
            list_ref[2 * block + 1, pos] = index
            at = tuple(at[b] + jnp.where(block == b, one, 0) for b in range(3))
        return at

    zero = jnp.int32(0)
    at = lax.fori_loop(0, LEAF, leaf_step, (zero, zero, zero))
    for b in range(3):
        n_ref[b] = at[b]
        for u in range(UNROLL):
            list_ref[2 * b, at[b] + u] = LEAF
            list_ref[2 * b + 1, at[b] + u] = 0


def leaf_rows(pack_ref, leaf):
    row = lax.broadcasted_iota(jnp.int32, (8, PTS), 0)
    out = jnp.zeros((8, PTS), f32)
    for c in range(3):
        line = jnp.concatenate(
            [pack_ref[15 + c, 2 * leaf:2 * leaf + 1, :], pack_ref[15 + c, 2 * leaf + 1:2 * leaf + 2, :]], axis=1
        )
        out = jnp.where(row == c, line, out)
    return out


def pieces(a):
    h = a.astype(bf16).astype(f32)
    r = a - h
    m = r.astype(bf16).astype(f32)
    return h, m, r - m


def near_kernel(block, first, last, list_ref, n_ref, own_ref, src_ref, x_ref, *refs):
    if first:
        acc_in = None
        out_ref, targets, centres, feats, xs, acc = refs
    else:
        acc_in, out_ref, targets, centres, feats, xs, acc = refs
    row = lax.broadcasted_iota(jnp.int32, (8, PTS), 0)
    eye = jnp.where(
        lax.broadcasted_iota(jnp.int32, (PTS, PTS), 0) == lax.broadcasted_iota(jnp.int32, (PTS, PTS), 1), 1.0, 0.0
    ).astype(bf16)
    for leaf in range(LEAF):
        targets[leaf] = leaf_rows(own_ref, leaf)
        source = leaf_rows(src_ref, leaf)
        centre = jnp.broadcast_to(jnp.sum(source, axis=1, keepdims=True) * (1.0 / PTS), (8, PTS))
        centres[leaf] = centre
        d = source - centre
        sq = jnp.sum(d * d, axis=0, keepdims=True) + smooth_sq
        h, m, l = pieces(jnp.where(row < 3, -2.0 * d, jnp.where(row == 3, 1.0, jnp.where(row == 4, sq, 0.0))))
        rows = jnp.concatenate([h, m, h, l, m, h, jnp.zeros((80, PTS), f32)], axis=0).astype(bf16)
        feats[leaf] = dot(eye, rows, NT).astype(bf16)
        xh, xl = split(x_ref[:, leaf * PTS:leaf * PTS + PTS] * inv_four_pi)
        xs[leaf] = jnp.concatenate([xh, xl], axis=0)
        if first:
            acc[leaf] = jnp.zeros((64, PTS), f32)
        else:
            acc[leaf] = acc_in[leaf]
    targets[LEAF] = jnp.zeros((8, PTS), f32)
    acc[LEAF] = jnp.zeros((64, PTS), f32)
    unit = jnp.where(row == 4, 1.0, 0.0)

    @pl.loop(0, (n_ref[block] + (UNROLL - 1)) // UNROLL)
    def _(i):
        ls = [list_ref[2 * block, i * UNROLL + u] for u in range(UNROLL)]
        js = [list_ref[2 * block + 1, i * UNROLL + u] for u in range(UNROLL)]
        dist = []
        for l, j in zip(ls, js):
            d = targets[l] - centres[j]
            sq = jnp.sum(d * d, axis=0, keepdims=True)
            h, m, low = pieces(jnp.where(row == 3, sq, d + unit))
            rows = jnp.concatenate([h, h, m, h, m, low], axis=0).astype(bf16)
            dist.append(dot(feats[j][:, :48], rows))
        for l, j, d2 in zip(ls, js, dist):
            kh, kl = split(lax.rsqrt(d2))
            x = xs[j]
            r = dot(x, kh) + dot(x, kl)
            acc[l] += r[:64] + r[64:]

    for leaf in range(LEAF):
        if last:
            out_ref[:, leaf * PTS:leaf * PTS + PTS] = acc[leaf]
        else:
            out_ref[leaf] = acc[leaf]


def far_kernel(
    far0_ref, far1_ref, far2_ref, p0_ref, p1_ref, p2_ref, tops_ref, c0_ref, c1_ref, c2_ref, t1_ref, t2_ref, basis_ref,
    acc_in, out_ref, q_ref,
):
    place = place_of()
    group = lax.axis_index("grp")
    for b, pack in enumerate((p0_ref, p1_ref, p2_ref)):
        for t in range(15):
            h, l = split(pack[t])
            q_ref[b * 15 + t] = jnp.concatenate([h, l], axis=0)

    def picked(tile, parity):
        half = lax.broadcasted_iota(jnp.int32, (128, 128), 1) // RANK
        return jnp.where(half == parity, tile, jnp.zeros_like(tile))

    def coupled(entries, weights):
        lhs = jnp.concatenate(
            [jnp.concatenate([picked(q_ref[tile], parity) for tile, parity in row], axis=1) for row in entries], axis=0
        )
        out = dot(lhs, wide_split(jnp.concatenate([w for w in weights for _ in range(2)], axis=0)))
        s = out[:, :128] + out[:, 128:]
        even, odd = s[0:64] + s[64:128], s[128:192] + s[192:256]
        return jnp.where(lanes_low(even.shape), even, odd)

    def entry(ref, target, f, width, base):
        block, index = relative(ref[target, f], place, width)
        return block * 15 + base + index // 2, lax.rem(index, 2)

    tiles = []
    for f in range(0, FAR2, 2):
        a = tops_ref[far2_ref[group, f]]
        b = tops_ref[far2_ref[group, f + 1]]
        a = jnp.concatenate([a, swap_halves(a)], axis=0)
        b = jnp.concatenate([swap_halves(b), b], axis=0)
        tiles.append(jnp.where(lanes_low(a.shape), a, b))
    th, tl = split(jnp.concatenate(tiles, axis=1))
    w = jnp.concatenate([c2_ref[f] for f in range(FAR2)], axis=0)
    wh, wl = split(jnp.concatenate([w, w], axis=1))
    y2 = dot(th, wh) + dot(tl, wh) + dot(th, wl)

    y1 = []
    for t in range(MID // 2):
        y = coupled(
            [[entry(far1_ref, 2 * t + i, f, MID, 12) for f in range(FAR1)] for i in range(2)],
            [c1_ref[f, :, t * 128:t * 128 + 128] for f in range(FAR1)],
        )
        w = t2_ref[:, t * 128:t * 128 + 128]
        even, odd = transposed(*halves(y2), jnp.concatenate([w, w], axis=0))
        y1.append(y + jnp.where(lanes_low(y.shape), even, odd))

    for t in range(LEAF // 2):
        y = coupled(
            [[entry(far0_ref, 2 * t + i, f, LEAF, 0) for f in range(FAR0)] for i in range(2)],
            [c0_ref[f, :, t * 128:t * 128 + 128] for f in range(FAR0)],
        )
        parent = y1[t // 4]
        other = swap_halves(parent)
        low = lanes_low(parent.shape)
        parent = jnp.where(low, parent, other) if (t // 2) % 2 == 0 else jnp.where(low, other, parent)
        w = t1_ref[:, t * 128:t * 128 + 128]
        even, odd = transposed(*halves(parent), jnp.concatenate([w, w], axis=0))
        y = y + jnp.where(low, even, odd)
        even, odd = transposed(*halves(y), basis_ref[:, t * 128:t * 128 + 128])
        out_ref[2 * t] = acc_in[2 * t] + even
        out_ref[2 * t + 1] = acc_in[2 * t + 1] + odd


VM = pl.BlockSpec(memory_space=pltpu.VMEM)
SM = pl.BlockSpec(memory_space=pltpu.SMEM)
PARAMS = pltpu.CompilerParams(vmem_limit_bytes=48 << 20)


def near_call(block, first, last, lists, counts, own, src, x, acc=None):
    shape = (64, LEAF * PTS) if last else (LEAF, 64, PTS)
    args = (lists, counts, own, src, x) + (() if first else (acc,))
    return pl.pallas_call(
        lambda *refs: near_kernel(block, first, last, *refs),
        out_shape=jax.ShapeDtypeStruct(shape, f32),
        in_specs=[SM, SM] + [VM] * (len(args) - 2),
        out_specs=VM,
        scratch_shapes=[
            pltpu.VMEM((LEAF + 1, 8, PTS), f32),
            pltpu.VMEM((LEAF, 8, PTS), f32),
            pltpu.VMEM((LEAF, PTS, 128), bf16),
            pltpu.VMEM((LEAF, 128, PTS), bf16),
            pltpu.VMEM((LEAF + 1, 64, PTS), f32),
        ],
        compiler_params=PARAMS,
        cost_estimate=pl.CostEstimate(flops=8_000_000_000, bytes_accessed=8_000_000, transcendentals=0),
        name="near_%d" % block,
    )(*args)


def local(
    coords, charges, basis, transfer1, transfer2, coupling0, coupling1, coupling2, near_list, near_count, far0_list,
    far1_list, far2_list,
):
    same_chip = [(i, i ^ 1) for i in range(DEVS)]
    next_chip = [(i, (i + (1 if i % 2 else DEVS - 1)) % DEVS) for i in range(DEVS)]
    x1 = lax.ppermute(charges, AXES, same_chip)
    x2 = lax.ppermute(charges, AXES, next_chip)
    pack, top, lists, counts = pl.pallas_call(
        up_kernel,
        out_shape=(
            jax.ShapeDtypeStruct((18, 64, 128), f32),
            jax.ShapeDtypeStruct((32, 128), f32),
            jax.ShapeDtypeStruct((6, LIST), jnp.int32),
            jax.ShapeDtypeStruct((4,), jnp.int32),
        ),
        in_specs=[SM, SM] + [VM] * 5,
        out_specs=(VM, VM, SM, SM),
        compiler_params=PARAMS,
        cost_estimate=pl.CostEstimate(flops=1_000_000_000, bytes_accessed=5_000_000, transcendentals=0),
        name="upward",
    )(near_list, near_count, coords, charges, basis, transfer1, transfer2)
    p1 = lax.ppermute(pack, AXES, same_chip)
    p2 = lax.ppermute(pack, AXES, next_chip)
    tops = lax.all_gather(lax.psum(top, "lane"), "grp", axis=0, tiled=False)
    acc = near_call(0, True, False, lists, counts, pack, pack, charges)
    acc = near_call(1, False, False, lists, counts, pack, p1, x1, acc)
    acc = pl.pallas_call(
        far_kernel,
        out_shape=jax.ShapeDtypeStruct((LEAF, 64, PTS), f32),
        in_specs=[SM] * 3 + [VM] * 11,
        out_specs=VM,
        scratch_shapes=[pltpu.VMEM((45, 128, 128), bf16)],
        compiler_params=PARAMS,
        cost_estimate=pl.CostEstimate(flops=3_000_000_000, bytes_accessed=10_000_000, transcendentals=0),
        name="downward",
    )(
        far0_list, far1_list, far2_list, pack, p1, p2, tops, coupling0, coupling1, coupling2, transfer1, transfer2,
        basis, acc,
    )
    return near_call(2, False, True, lists, counts, pack, p2, x2, acc)


def solution(mesh):
    placed = (
        P(None, AXES),
        P(None, AXES),
        P(None, AXES),
        P(None, AXES),
        P(None, AXES),
        P(None, None, AXES),
        P(None, None, AXES),
        P(None, None, "grp"),
        P(AXES, None),
        P(AXES),
        P(AXES, None),
        P(AXES, None),
        P(),
    )
    return jax.shard_map(local, mesh=mesh, in_specs=placed, out_specs=P(None, AXES), check_vma=False)
```

profile of v0, /device:TPU:0, one launch (start us, length us, event | category | flops | bytes accessed | tf_op | source)
XLA Modules:
  0.0 130.1 jit_solution(9975455870527899534)
XLA Ops:
  0.0 0.0 collective-permute-start.3
  0.0 0.8 copy.18.near_ref
  0.8 1.4 %copy-done = f32[256,1536]{1,0:T(8,128)S(1)} copy-done((f32[256,1536]{1,0:T(8,128)S(1)}, f32[256,1536]{1,0:T(8,128)}, u32[]{:S(2)}) %copy-start) | copy-done | bytes 1572888
  2.2 1.0 copy-done.2
  3.2 0.9 copy-done.4
  4.1 0.9 copy-done.5
  5.0 0.7 copy-done.7
  5.6 8.4 %upward.1 = (f32[18,64,128]{2,1,0:T(8,128)}, f32[32,128]{1,0:T(8,128)S(1)}, s32[6,256]{1,0:T(8,128)S(1)}, s32[4]{0:T(128)S(1)}) custom-call(s32[24,9]{1,0:T(8,128)S(1)} %copy.18.near_ref, s32[24]{0:T(128)S(1)} %copy-done.7, f32[3,6144]{1,0:T(4,128)S(1)} %copy-done.4, f32[64,6144]{1,0:T(8,128)} %refs_4_.1, f32[256,1536]{1,0:T(8,128)S(1)} %copy-done, ...), custom_call_target="tpu_custom_call" | custom-call | flops 1000000000 | bytes 5000000 | tf_op jit(solution)/shard_map/upward/pallas_call | solution.py:323
  14.1 0.6 collective-permute-start.2
  14.7 8.5 %collective-permute-start = (f32[18,64,128]{2,1,0:T(8,128)}, f32[18,64,128]{2,1,0:T(8,128)}, u32[]{:S(2)}, u32[]{:S(2)}) collective-permute-start(f32[18,64,128]{2,1,0:T(8,128)} %get-tuple-element.11.refs_2_.refs_3_.p0_ref), channel_id=1, source_target_pairs={{0,127},{1,2},{2,1},{3,4},{4,3},{5,6},{6,5},{7,8},{8,7},{9,10},{10... | collective-permute-start | bytes 1769480 | tf_op jit(solution)/shard_map/ppermute | solution.py:338
  23.1 0.1 collective-permute-start.1
  23.2 0.0 copy-done.11
  23.2 0.1 copy.19.far0_ref
  23.3 0.1 copy.21.far2_ref
  23.4 0.1 copy.20.far1_ref
  23.5 35.6 %psum.7 = f32[1,32,128]{2,1,0:T(8,128)S(1)} all-reduce(f32[1,32,128]{2,1,0:T(8,128)S(1)} %bitcast.1), channel_id=1, replica_groups=mesh['grp'=16,'lane'=8] {'lane'}, use_global_device_ids=true, to_apply=%region_0.0 | all-reduce | flops 4096 | bytes 32768 | tf_op jit(solution)/shard_map/psum | solution.py:339
  59.1 27.5 %all_gather.7.tops_ref = f32[16,32,128]{2,1,0:T(8,128)S(1)} all-gather(f32[1,32,128]{2,1,0:T(8,128)S(1)} %psum.7), channel_id=1, replica_groups=mesh['grp'=16,'lane'=8] {'grp'}, dimensions={0}, use_global_device_ids=true | all-gather | bytes 278528 | tf_op jit(solution)/shard_map/all_gather | solution.py:339
  86.5 13.5 %near_0.1.refs_5_ = f32[24,64,256]{2,1,0:T(8,128)S(1)} custom-call(s32[6,256]{1,0:T(8,128)S(1)} %get-tuple-element.9.refs_0_, s32[4]{0:T(128)S(1)} %get-tuple-element.10.refs_1_, f32[18,64,128]{2,1,0:T(8,128)} %get-tuple-element.11.refs_2_.refs_3_.p0_ref, f32[18,64,128]{2,1,0:T(8,128)} %get-tuple-element.11.refs_2_.refs_3_.p0_ref, f32[64,6144]{1,0:T(8,128)} %refs_4_.1), custom_call_target="tpu_custom_call" | custom-call | flops 8000000000 | bytes 8000000 | tf_op jit(solution)/shard_map/near_0/pallas_call | solution.py:297
  100.0 0.0 copy-start.1
  100.1 0.0 copy-start.3
  100.1 0.0 copy-start.6
  100.1 0.0 copy-start.8
  100.1 0.0 copy-start.9
  100.1 0.0 collective-permute-done.2.refs_3_.p1_ref
  100.1 0.0 collective-permute-done.3.refs_4_
  100.1 9.8 %near_1.1.acc_in = f32[24,64,256]{2,1,0:T(8,128)S(1)} custom-call(s32[6,256]{1,0:T(8,128)S(1)} %get-tuple-element.9.refs_0_, s32[4]{0:T(128)S(1)} %get-tuple-element.10.refs_1_, f32[18,64,128]{2,1,0:T(8,128)} %get-tuple-element.11.refs_2_.refs_3_.p0_ref, f32[18,64,128]{2,1,0:T(8,128)} %collective-permute-done.2.refs_3_.p1_ref, ...), custom_call_target="tpu_custom_call" | custom-call | flops 8000000000 | bytes 8000000 | tf_op jit(solution)/shard_map/near_1/pallas_call | solution.py:297
  109.9 0.0 copy-start.10
  109.9 1.1 copy-done.10
  111.1 0.0 collective-permute-done.p2_ref.refs_3_
  111.1 9.6 %downward.1.refs_5_ = f32[24,64,256]{2,1,0:T(8,128)S(1)} custom-call(s32[24,8]{1,0:T(8,128)S(1)} %copy.19.far0_ref, s32[6,4]{1,0:T(8,128)S(1)} %copy.20.far1_ref, s32[16,4]{1,0:T(8,128)S(1)} %copy.21.far2_ref, f32[18,64,128]{2,1,0:T(8,128)} %get-tuple-element.11.refs_2_.refs_3_.p0_ref, f32[18,64,128]{2,1,0:T(8,128)} %collective-permute-done.2.refs_3_.p1_ref, ...), custom_call_target="tpu_custom_call" | custom-call | flops 3000000000 | bytes 10000000 | tf_op jit(solution)/shard_map/downward/pallas_call | solution.py:342
  120.7 0.0 collective-permute-done.1.refs_4_
  120.7 9.4 %near_2.1 = f32[64,6144]{1,0:T(8,128)} custom-call(s32[6,256]{1,0:T(8,128)S(1)} %get-tuple-element.9.refs_0_, s32[4]{0:T(128)S(1)} %get-tuple-element.10.refs_1_, f32[18,64,128]{2,1,0:T(8,128)} %get-tuple-element.11.refs_2_.refs_3_.p0_ref, f32[18,64,128]{2,1,0:T(8,128)} %collective-permute-done.p2_ref.refs_3_, ...), custom_call_target="tpu_custom_call" | custom-call | flops 8000000000 | bytes 8000000 | tf_op jit(solution)/shard_map/near_2/pallas_call | solution.py:297
  (15 shorter events, 0.0 us)
Async XLA Ops:
  0.0 100.1 %collective-permute-start.3 = (f32[64,6144]{1,0:T(8,128)}, f32[64,6144]{1,0:T(8,128)S(1)}, u32[]{:S(2)}, u32[]{:S(2)}) collective-permute-start(f32[64,6144]{1,0:T(8,128)} %refs_4_.1), channel_id=1, source_target_pairs={{0,1},{1,0},{2,3},{3,2},{4,5},{5,4},{6,7},{7,6},{8,9},{9,8},{10,11... | collective-permute-start | bytes 4718600 | tf_op jit(solution)/shard_map/ppermute | solution.py:321
  0.8 1.4 %copy-start = (f32[256,1536]{1,0:T(8,128)S(1)}, f32[256,1536]{1,0:T(8,128)}, u32[]{:S(2)}) copy-start(f32[256,1536]{1,0:T(8,128)} %basis_ref.3) | copy-start | bytes 4718596
  2.2 1.0 copy-start.2
  3.2 0.9 copy-start.4
  4.1 0.9 copy-start.5
  5.0 0.7 copy-start.7
  5.6 17.6 %copy-start.11 = (s32[24,8]{0,1:T(8,128)S(1)}, s32[24,8]{0,1:T(8,128)}, u32[]{:S(2)}) copy-start(s32[24,8]{0,1:T(8,128)} %param.23) | copy-start | bytes 2308
  5.6 17.7 %copy-start.12 = (s32[16,4]{0,1:T(4,128)S(1)}, s32[16,4]{0,1:T(4,128)}, u32[]{:S(2)}) copy-start(s32[16,4]{0,1:T(4,128)} %param.25) | copy-start | bytes 772
  5.6 17.7 %copy-start.13 = (s32[6,4]{0,1:T(4,128)S(1)}, s32[6,4]{0,1:T(4,128)}, u32[]{:S(2)}) copy-start(s32[6,4]{0,1:T(4,128)} %param.24) | copy-start | bytes 292
  14.1 86.0 %collective-permute-start.2 = (f32[18,64,128]{2,1,0:T(8,128)}, f32[18,64,128]{2,1,0:T(8,128)}, u32[]{:S(2)}, u32[]{:S(2)}) collective-permute-start(f32[18,64,128]{2,1,0:T(8,128)} %get-tuple-element.11.refs_2_.refs_3_.p0_ref), channel_id=1, source_target_pairs={{0,1},{1,0},{2,3},{3,2},{4,5},{5,4},{6,7},{7,6},{8,9},{9,8},{10,11... | collective-permute-start | bytes 1769480 | tf_op jit(solution)/shard_map/ppermute | solution.py:337
  14.7 96.4 %collective-permute-start = (f32[18,64,128]{2,1,0:T(8,128)}, f32[18,64,128]{2,1,0:T(8,128)}, u32[]{:S(2)}, u32[]{:S(2)}) collective-permute-start(f32[18,64,128]{2,1,0:T(8,128)} %get-tuple-element.11.refs_2_.refs_3_.p0_ref), channel_id=1, source_target_pairs={{0,127},{1,2},{2,1},{3,4},{4,3},{5,6},{6,5},{7,8},{8,7},{9,10},{10... | collective-permute-start | bytes 1769480 | tf_op jit(solution)/shard_map/ppermute | solution.py:338
  23.1 97.6 %collective-permute-start.1 = (f32[64,6144]{1,0:T(8,128)}, f32[64,6144]{1,0:T(8,128)S(1)}, u32[]{:S(2)}, u32[]{:S(2)}) collective-permute-start(f32[64,6144]{1,0:T(8,128)} %refs_4_.1), channel_id=1, source_target_pairs={{0,127},{1,2},{2,1},{3,4},{4,3},{5,6},{6,5},{7,8},{8,7},{9,10},{10... | collective-permute-start | bytes 4718600 | tf_op jit(solution)/shard_map/ppermute | solution.py:322
  100.0 11.0 %copy-start.1 = (f32[256,1536]{1,0:T(8,128)S(1)}, f32[256,1536]{1,0:T(8,128)}, u32[]{:S(2)}) copy-start(f32[256,1536]{1,0:T(8,128)} %basis_ref.3) | copy-start | bytes 4718596
  100.1 11.0 %copy-start.3 = (f32[64,1536]{1,0:T(8,128)S(1)}, f32[64,1536]{1,0:T(8,128)}, u32[]{:S(2)}) copy-start(f32[64,1536]{1,0:T(8,128)} %t1_ref.3) | copy-start | bytes 1179652
  100.1 11.0 %copy-start.6 = (f32[64,384]{1,0:T(8,128)S(1)}, f32[64,384]{1,0:T(8,128)}, u32[]{:S(2)}) copy-start(f32[64,384]{1,0:T(8,128)} %t2_ref.3) | copy-start | bytes 294916
  100.1 11.0 %copy-start.8 = (f32[4,64,384]{2,1,0:T(8,128)S(1)}, f32[4,64,384]{2,1,0:T(8,128)}, u32[]{:S(2)}) copy-start(f32[4,64,384]{2,1,0:T(8,128)} %c1_ref.1) | copy-start | bytes 1179652
  100.1 11.0 %copy-start.9 = (f32[4,64,64]{2,1,0:T(8,128)S(1)}, f32[4,64,64]{2,1,0:T(8,128)}, u32[]{:S(2)}) copy-start(f32[4,64,64]{2,1,0:T(8,128)} %c2_ref.1) | copy-start | bytes 196612
  109.9 1.1 copy-start.10
where the time goes:
time: 131 us; the launch traced here: 130 us
  blocking collectives  63.1 us (48%)
  Pallas kernels  50.7 us (39%)
  starting transfers between devices  9.14 us (7%)
  local copies, waits for them, and re-layouts  7.04 us (5%)
    psum x1, blocking collectives, local(): tops = lax.all_gather(lax.psum(top, 'lane'), 'grp', axis=0, tiled=False)  35.6 us
    pallas_call x3, Pallas kernels, near_call(): pl.pallas_call(lambda *refs: near_kernel(block, first, last, *refs), out_...  32.7 us
    all_gather x1, blocking collectives, local(): tops = lax.all_gather(lax.psum(top, 'lane'), 'grp', axis=0, tiled=False)  27.5 us
    pallas_call x1, Pallas kernels, local(): pl.pallas_call(far_kernel, out_shape=jax.ShapeDtypeStruct((LEAF, 64, PTS)...  9.56 us
    ppermute x1, starting transfers between devices, local(): p2 = lax.ppermute(pack, AXES, next_chip)  8.46 us
    pallas_call x1, Pallas kernels, local(): pl.pallas_call(up_kernel, out_shape=(jax.ShapeDtypeStruct((18, 64, 128),...  8.43 us
    unnamed x32, local copies, waits for them, and re-layouts  7.04 us
  transfers between devices with their start and end apart: 4, of which 0 were waited for; matrix products, arithmetic and copies ran while one was open for 1% of the time, Pallas kernels for 32%

commit v1 on v0

v1 whole, which is shorter than its diff:
```python
import math

import jax
import jax.numpy as jnp
from jax import lax
from jax.experimental import pallas as pl
from jax.experimental.pallas import tpu as pltpu
from jax.sharding import PartitionSpec as P

AXES = ("grp", "lane")
LANES = 8
DEVS = 128
LEAF = 24
MID = 6
PTS = 256
RANK = 64
NEAR = 9
FAR0 = 8
FAR1 = 4
FAR2 = 4
UNROLL = 12
LIST = 512
SLOTS = 5
COUNT_AT = 127
REST_AT = 128
GROUPS = 16
MESH = pl.DeviceIdType.MESH
inv_four_pi = 1.0 / (4.0 * math.pi)
smooth_sq = 5e-05
bf16 = jnp.bfloat16
f32 = jnp.float32
NT = (((1,), (1,)), ((), ()))


def dot(a, b, dims=(((1,), (0,)), ((), ()))):
    return lax.dot_general(a, b, dims, preferred_element_type=f32)


def split(a):
    high = a.astype(bf16)
    return high, (a - high.astype(f32)).astype(bf16)


def lanes_low(shape):
    return lax.broadcasted_iota(jnp.int32, shape, len(shape) - 1) < RANK


def swap_halves(a):
    return pltpu.roll(a, RANK, 1)


def halves(tile):
    low = lanes_low(tile.shape)
    return jnp.where(low, tile, 0.0), jnp.where(low, 0.0, tile)


def place_of():
    return lax.axis_index("grp") * LANES + lax.axis_index("lane")


def relative(entry, place, width):
    rel = lax.rem(entry - place * width + (DEVS + 1) * width, DEVS * width)
    cat = rel // width
    index = rel - cat * width
    other = jnp.where(lax.rem(place, 2) == 0, 2, 0)
    block = jnp.where(cat == 1, 0, jnp.where(cat == other, 1, 2))
    return block, index


def stacked_split(rows_a, rows_b):
    ah, al = split(rows_a)
    bh, bl = split(rows_b)
    return jnp.concatenate([ah, bh, al, bl], axis=0)


def wide_split(a):
    h, l = split(a)
    return jnp.concatenate([h, l], axis=1)


def fold(out):
    s = out[:, :128] + out[:, 128:]
    return s[0:64] + s[128:192], s[64:128] + s[192:256]


def transposed(rows_a, rows_b, weights):
    lhs = stacked_split(rows_a, rows_b)
    wh, wl = split(weights)
    r = dot(lhs, wh, NT)
    r2 = dot(lhs[:128], wl, NT)
    return r[0:64] + r[128:192] + r2[0:64], r[64:128] + r[192:256] + r2[64:128]


def list_kernel(near_ref, count_ref, list_ref):
    place = place_of()
    even = lax.rem(place, 2) == 0
    low_off = jnp.where(even, 72, 48)
    high_off = jnp.where(even, 0, 24)

    def leaf_step(leaf, pos):
        live = count_ref[leaf]
        list_ref[leaf * SLOTS] = leaf
        for s in range(1, SLOTS):
            list_ref[leaf * SLOTS + s] = LEAF
        own_at = leaf * SLOTS + 1
        own_end = leaf * SLOTS + SLOTS
        for k in range(1, NEAR):
            rel = near_ref[leaf, k] - place * LEAF
            rel = jnp.where(rel < -LEAF, rel + DEVS * LEAF, jnp.where(rel >= 2 * LEAF, rel - DEVS * LEAF, rel))
            near_side = jnp.logical_and(rel >= 0, rel < LEAF)
            source = rel + jnp.where(near_side, 0, jnp.where(rel < 0, low_off, high_off))
            here = jnp.logical_and(jnp.logical_and(near_side, own_at < own_end), live > k)
            list_ref[jnp.where(here, own_at, REST_AT + pos)] = jnp.where(here, source, leaf * 128 + source)
            own_at = own_at + jnp.where(here, 1, 0)
            pos = pos + jnp.where(jnp.logical_and(live > k, jnp.logical_not(here)), 1, 0)
        return pos

    pos = lax.fori_loop(0, LEAF, leaf_step, jnp.int32(0))
    list_ref[COUNT_AT] = pos
    for u in range(UNROLL):
        list_ref[REST_AT + pos + u] = LEAF * 128


def upward(coords_ref, x_ref, basis_ref, t1_ref, t2_ref, pack_ref):
    tiles = []
    for t in range(LEAF // 2):
        xa = x_ref[:, t * 512:t * 512 + 256]
        xb = x_ref[:, t * 512 + 256:t * 512 + 512]
        ra, rb = fold(dot(stacked_split(xa, xb), wide_split(basis_ref[:, t * 128:t * 128 + 128])))
        q = jnp.where(lanes_low(ra.shape), ra, rb)
        pack_ref[t] = q
        tiles.append(q)
    mids = []
    parts = []
    for m in range(MID):
        a0, b0 = halves(tiles[2 * m])
        a1, b1 = halves(tiles[2 * m + 1])
        e0 = t1_ref[:, m * 256:m * 256 + 128]
        e1 = t1_ref[:, m * 256 + 128:m * 256 + 256]
        lhs = stacked_split(jnp.concatenate([a0, a1], axis=1), jnp.concatenate([b0, b1], axis=1))
        parts.append(fold(dot(lhs, wide_split(jnp.concatenate([e0, e0, e1, e1], axis=0)))))
    for t in range(MID // 2):
        (top0, bot0), (top1, bot1) = parts[2 * t], parts[2 * t + 1]
        low = lanes_low(top0.shape)
        mid = jnp.where(low, top0, bot1) + swap_halves(jnp.where(low, top1, bot0))
        pack_ref[LEAF // 2 + t] = mid
        mids.append(mid)
    both = [halves(m) for m in mids]
    weights = [t2_ref[:, t * 128:t * 128 + 128] for t in range(MID // 2)]
    lhs = stacked_split(
        jnp.concatenate([b[0] for b in both], axis=1), jnp.concatenate([b[1] for b in both], axis=1)
    )
    top, bot = fold(dot(lhs, wide_split(jnp.concatenate([w for w in weights for _ in range(2)], axis=0))))
    for i in range(2 * LEAF):
        for c in range(3):
            pack_ref[15 + c, i:i + 1, :] = coords_ref[c:c + 1, i * 128:i * 128 + 128]
    zero = jnp.zeros((16, 128), f32)
    for c in range(3):
        pack_ref[15 + c, 48:64, :] = zero
    s = jnp.where(lanes_low(top.shape), top, bot)
    return s + swap_halves(s)


def leaf_rows(pack_ref, leaf):
    row = lax.broadcasted_iota(jnp.int32, (8, PTS), 0)
    out = jnp.zeros((8, PTS), f32)
    for c in range(3):
        line = jnp.concatenate(
            [pack_ref[15 + c, 2 * leaf:2 * leaf + 1, :], pack_ref[15 + c, 2 * leaf + 1:2 * leaf + 2, :]], axis=1
        )
        out = jnp.where(row == c, line, out)
    return out


def pieces(a):
    h = a.astype(bf16).astype(f32)
    r = a - h
    m = r.astype(bf16).astype(f32)
    return h, m, r - m


def identity():
    return jnp.where(
        lax.broadcasted_iota(jnp.int32, (PTS, PTS), 0) == lax.broadcasted_iota(jnp.int32, (PTS, PTS), 1), 1.0, 0.0
    ).astype(bf16)


def prepare(pack_ref, x_ref, leaf, at, eye, centres, feats, xs):
    row = lax.broadcasted_iota(jnp.int32, (8, PTS), 0)
    source = leaf_rows(pack_ref, leaf)
    centre = jnp.broadcast_to(jnp.sum(source, axis=1, keepdims=True) * (1.0 / PTS), (8, PTS))
    centres[at] = centre
    d = source - centre
    sq = jnp.sum(d * d, axis=0, keepdims=True) + smooth_sq
    h, m, l = pieces(jnp.where(row < 3, -2.0 * d, jnp.where(row == 3, 1.0, jnp.where(row == 4, sq, 0.0))))
    rows = jnp.concatenate([h, m, h, l, m, h, jnp.zeros((80, PTS), f32)], axis=0).astype(bf16)
    feats[at] = dot(eye, rows, NT).astype(bf16)
    xh, xl = split(x_ref[:, leaf * PTS:leaf * PTS + PTS] * inv_four_pi)
    xs[at] = jnp.concatenate([xh, xl], axis=0)


def pairs(ls, js, targets, centres, feats, xs, acc):
    unit = jnp.where(lax.broadcasted_iota(jnp.int32, (8, PTS), 0) == 4, 1.0, 0.0)
    row = lax.broadcasted_iota(jnp.int32, (8, PTS), 0)
    dist = []
    for l, j in zip(ls, js):
        d = targets[l] - centres[j]
        sq = jnp.sum(d * d, axis=0, keepdims=True)
        h, m, low = pieces(jnp.where(row == 3, sq, d + unit))
        rows = jnp.concatenate([h, h, m, h, m, low], axis=0).astype(bf16)
        dist.append(dot(feats[j][:, :48], rows))
    for l, j, d2 in zip(ls, js, dist):
        kh, kl = split(lax.rsqrt(d2))
        x = xs[j]
        r = dot(x, kh) + dot(x, kl)
        acc[l] += r[:64] + r[64:]


def first_kernel(
    list_ref, far2_ref, coords_hbm, x_hbm, basis_hbm, t1_hbm, t2_hbm, c2_ref,
    acc_ref, pack_ref, p1_ref, p2_ref, x1_ref, x2_ref, y2_ref, centres, feats, xs,
    coords, x, basis, t1, t2, targets, parts, parts_in, mine, slices, y2_mine, y2_in,
    load_sem, part_send, part_recv, slice_send, slice_recv, y2_send, y2_recv, near_send, near_recv,
):
    group = lax.axis_index("grp")
    lane = lax.axis_index("lane")
    place = group * LANES + lane
    even = lax.rem(lane, 2) == 0
    partner = (group, lane + 1 - 2 * lax.rem(lane, 2))
    beyond = lax.rem(place + jnp.where(even, DEVS - 1, 1), DEVS)
    beyond = (beyond // LANES, lax.rem(beyond, LANES))
    loads = [
        pltpu.make_async_copy(src, dst, load_sem.at[i])
        for i, (src, dst) in enumerate(
            [(x_hbm.at[:, c * 1536:c * 1536 + 1536], x.at[:, c * 1536:c * 1536 + 1536]) for c in range(4)]
            + [(basis_hbm.at[r * 64:r * 64 + 64], basis.at[r * 64:r * 64 + 64]) for r in range(4)]
            + [(t1_hbm, t1), (t2_hbm, t2), (coords_hbm, coords)]
        )
    ]
    for c in loads:
        c.start()
    barrier = pltpu.get_barrier_semaphore()
    for d in range(1, LANES):
        pl.semaphore_signal(barrier, inc=1, device_id=(group, lax.rem(lane + d, LANES)), device_id_type=MESH)
    for d in range(1, GROUPS):
        pl.semaphore_signal(barrier, inc=1, device_id=(lax.rem(group + d, GROUPS), lane), device_id_type=MESH)
    pl.semaphore_signal(barrier, inc=1, device_id=beyond, device_id_type=MESH)
    for c in loads:
        c.wait()
    top = upward(coords, x, basis, t1, t2, pack_ref)
    for r in range(LANES):
        parts[r] = top[r * 8:r * 8 + 8]
    pl.semaphore_wait(barrier, LANES + GROUPS - 1)

    def part_copy(d):
        peer = lax.rem(lane + d, LANES)
        return pltpu.make_async_remote_copy(
            parts.at[peer], parts_in.at[lane], part_send.at[d], part_recv.at[lane], (group, peer), MESH
        ), pltpu.make_async_remote_copy(
            parts.at[peer], parts_in.at[peer], part_send.at[d], part_recv.at[peer], (group, peer), MESH
        )

    def slice_copy(d):
        peer = lax.rem(group + d, GROUPS)
        return pltpu.make_async_remote_copy(
            mine, slices.at[group], slice_send.at[d], slice_recv.at[group], (peer, lane), MESH
        ), pltpu.make_async_remote_copy(
            mine, slices.at[peer], slice_send.at[d], slice_recv.at[peer], (peer, lane), MESH
        )

    def y2_copy(d):
        peer = lax.rem(lane + d, LANES)
        return pltpu.make_async_remote_copy(
            y2_mine, y2_in.at[lane], y2_send.at[d], y2_recv.at[lane], (group, peer), MESH
        ), pltpu.make_async_remote_copy(
            y2_mine, y2_in.at[peer], y2_send.at[d], y2_recv.at[peer], (group, peer), MESH
        )

    for d in range(1, LANES):
        part_copy(d)[0].start()
    swaps = [
        pltpu.make_async_remote_copy(src, dst, near_send.at[i], near_recv.at[i], dev, MESH)
        for i, (src, dst, dev) in enumerate(
            [(pack_ref, p2_ref, beyond), (pack_ref, p1_ref, partner), (x_hbm, x1_ref, partner)]
        )
    ]
    back = pltpu.make_async_remote_copy(x_hbm, x2_ref, near_send.at[3], near_recv.at[3], beyond, MESH)
    for c in swaps:
        c.start()

    @pl.when(even)
    def _():
        back.start()

    eye = identity()
    for leaf in range(LEAF):
        targets[leaf] = leaf_rows(pack_ref, leaf)
        prepare(pack_ref, x, leaf, leaf, eye, centres, feats, xs)
        acc_ref[leaf] = jnp.zeros((64, PTS), f32)
    centres[LEAF] = jnp.zeros((8, PTS), f32)
    feats[LEAF] = feats[0]
    xs[LEAF] = jnp.zeros((128, PTS), bf16)

    def leaves(i, _):
        ls = [2 * i + u for u in range(2) for s in range(SLOTS)]
        js = [list_ref[(2 * i + u) * SLOTS + s] for u in range(2) for s in range(SLOTS)]
        pairs(ls, js, targets, centres, feats, xs, acc_ref)
        return 0

    for d in range(1, LANES):
        part_copy(d)[1].wait_recv()
    parts_in[lane] = parts[lane]
    total = parts_in[0]
    for r in range(1, LANES):
        total = total + parts_in[r]
    mine[...] = total
    slices[group] = total
    for d in range(1, GROUPS):
        slice_copy(d)[0].start()

    lax.fori_loop(0, 4, leaves, 0)

    for d in range(1, GROUPS):
        slice_copy(d)[1].wait_recv()
    low = lanes_low((8, 128))
    picks = [slices[far2_ref[group, f]] for f in range(FAR2)]
    rows = jnp.concatenate([jnp.where(low, picks[f], picks[f + 1]) for f in range(0, FAR2, 2)], axis=1)
    w = jnp.concatenate([c2_ref[f] for f in range(FAR2)], axis=0)
    wh, wl = split(jnp.concatenate([w, w], axis=1))
    rh, rl = split(rows)
    y2 = dot(rh, wh) + dot(rl, wh) + dot(rh, wl)
    y2_mine[...] = y2
    y2_in[lane] = y2
    for d in range(1, LANES):
        y2_copy(d)[0].start()

    lax.fori_loop(4, LEAF // 2, leaves, 0)

    for d in range(1, LANES):
        y2_copy(d)[1].wait_recv()
    for r in range(LANES):
        y2_ref[r * 8:r * 8 + 8, :] = y2_in[r]
    for d in range(1, LANES):
        part_copy(d)[0].wait_send()
        y2_copy(d)[0].wait_send()
    for d in range(1, GROUPS):
        slice_copy(d)[0].wait_send()
    for c in swaps:
        c.wait()

    @pl.when(even)
    def _():
        back.wait_send()

    @pl.when(jnp.logical_not(even))
    def _():
        back.wait_recv()


def rest_kernel(
    list_ref, own_ref, p1_ref, p2_ref, own_centres, own_feats, own_xs, x1_hbm, x2_hbm, x3_hbm, acc_in, out_ref,
    targets, centres, feats, xs, acc, x, sem,
):
    even = lax.rem(lax.axis_index("lane"), 2) == 0

    def load(src, i):
        return pltpu.make_async_copy(src, x.at[i], sem.at[i])

    load(x1_hbm, 0).start()

    @pl.when(even)
    def _():
        load(x3_hbm, 1).start()

    @pl.when(jnp.logical_not(even))
    def _():
        load(x2_hbm, 1).start()

    moves = [
        pltpu.make_async_copy(own_feats.at[0:LEAF], feats.at[0:LEAF], sem.at[2]),
        pltpu.make_async_copy(own_xs.at[0:LEAF], xs.at[0:LEAF], sem.at[3]),
    ]
    for c in moves:
        c.start()
    for leaf in range(LEAF):
        targets[leaf] = leaf_rows(own_ref, leaf)
        centres[leaf] = own_centres[leaf]
        acc[leaf] = acc_in[leaf]
    targets[LEAF] = jnp.zeros((8, PTS), f32)
    acc[LEAF] = jnp.zeros((64, PTS), f32)
    eye = identity()
    for b, pack in enumerate((p1_ref, p2_ref)):
        load(x1_hbm, b).wait()
        for leaf in range(LEAF):
            prepare(pack, x.at[b], leaf, LEAF * (b + 1) + leaf, eye, centres, feats, xs)
    for c in moves:
        c.wait()

    @pl.loop(0, (list_ref[COUNT_AT] + (UNROLL - 1)) // UNROLL)
    def _(i):
        words = [list_ref[REST_AT + i * UNROLL + u] for u in range(UNROLL)]
        pairs([w // 128 for w in words], [lax.rem(w, 128) for w in words], targets, centres, feats, xs, acc)

    for leaf in range(LEAF):
        out_ref[:, leaf * PTS:leaf * PTS + PTS] = acc[leaf]


def far_kernel(
    far0_ref, far1_ref, p0_ref, p1_ref, p2_ref, y2_ref, c0_ref, c1_ref, t1_ref, t2_ref, basis_ref,
    acc_in, out_ref, q_ref,
):
    place = place_of()
    for b, pack in enumerate((p0_ref, p1_ref, p2_ref)):
        for t in range(15):
            h, l = split(pack[t])
            q_ref[b * 15 + t] = jnp.concatenate([h, l], axis=0)

    def picked(tile, parity):
        half = lax.broadcasted_iota(jnp.int32, (128, 128), 1) // RANK
        return jnp.where(half == parity, tile, jnp.zeros_like(tile))

    def coupled(entries, weights):
        lhs = jnp.concatenate(
            [jnp.concatenate([picked(q_ref[tile], parity) for tile, parity in row], axis=1) for row in entries], axis=0
        )
        out = dot(lhs, wide_split(jnp.concatenate([w for w in weights for _ in range(2)], axis=0)))
        s = out[:, :128] + out[:, 128:]
        even, odd = s[0:64] + s[64:128], s[128:192] + s[192:256]
        return jnp.where(lanes_low(even.shape), even, odd)

    def entry(ref, target, f, width, base):
        block, index = relative(ref[target, f], place, width)
        return block * 15 + base + index // 2, lax.rem(index, 2)

    y2 = y2_ref[...]
    y1 = []
    for t in range(MID // 2):
        y = coupled(
            [[entry(far1_ref, 2 * t + i, f, MID, 12) for f in range(FAR1)] for i in range(2)],
            [c1_ref[f, :, t * 128:t * 128 + 128] for f in range(FAR1)],
        )
        w = t2_ref[:, t * 128:t * 128 + 128]
        even, odd = transposed(*halves(y2), jnp.concatenate([w, w], axis=0))
        y1.append(y + jnp.where(lanes_low(y.shape), even, odd))

    for t in range(LEAF // 2):
        y = coupled(
            [[entry(far0_ref, 2 * t + i, f, LEAF, 0) for f in range(FAR0)] for i in range(2)],
            [c0_ref[f, :, t * 128:t * 128 + 128] for f in range(FAR0)],
        )
        parent = y1[t // 4]
        other = swap_halves(parent)
        low = lanes_low(parent.shape)
        parent = jnp.where(low, parent, other) if (t // 2) % 2 == 0 else jnp.where(low, other, parent)
        w = t1_ref[:, t * 128:t * 128 + 128]
        even, odd = transposed(*halves(parent), jnp.concatenate([w, w], axis=0))
        y = y + jnp.where(low, even, odd)
        even, odd = transposed(*halves(y), basis_ref[:, t * 128:t * 128 + 128])
        out_ref[2 * t] = acc_in[2 * t] + even
        out_ref[2 * t + 1] = acc_in[2 * t + 1] + odd


VM = pl.BlockSpec(memory_space=pltpu.VMEM)
SM = pl.BlockSpec(memory_space=pltpu.SMEM)
ANY = pl.BlockSpec(memory_space=pl.ANY)
DMA = pltpu.SemaphoreType.DMA


def params(mib, **more):
    return pltpu.CompilerParams(vmem_limit_bytes=mib << 20, **more)


def cost(size):
    return pl.CostEstimate(flops=size, bytes_accessed=1000, transcendentals=0)


def shape(*dims, dtype=f32):
    return jax.ShapeDtypeStruct(dims, dtype)


def local(
    coords, charges, basis, transfer1, transfer2, coupling0, coupling1, coupling2, near_list, near_count, far0_list,
    far1_list, far2_list,
):
    x3 = lax.ppermute(charges, AXES, [(i, (i + 1) % DEVS) for i in range(1, DEVS, 2)])
    lists = pl.pallas_call(
        list_kernel, out_shape=shape(LIST, dtype=jnp.int32), in_specs=[SM, SM], out_specs=SM, cost_estimate=cost(1000),
        name="lists",
    )(near_list, near_count)
    acc, pack, p1, p2, x1, x2, y2, centres, feats, xs = pl.pallas_call(
        first_kernel,
        out_shape=(
            shape(LEAF, 64, PTS), shape(18, 64, 128), shape(18, 64, 128), shape(18, 64, 128), shape(64, LEAF * PTS),
            shape(64, LEAF * PTS), shape(64, 128), shape(LEAF + 1, 8, PTS), shape(LEAF + 1, PTS, 128, dtype=bf16),
            shape(LEAF + 1, 128, PTS, dtype=bf16),
        ),
        in_specs=[SM, SM] + [ANY] * 5 + [VM],
        out_specs=(VM, VM, ANY, ANY, ANY, ANY, VM, VM, VM, VM),
        scratch_shapes=[
            pltpu.VMEM((3, LEAF * PTS), f32), pltpu.VMEM((64, LEAF * PTS), f32), pltpu.VMEM((PTS, LEAF * RANK), f32),
            pltpu.VMEM((RANK, LEAF * RANK), f32), pltpu.VMEM((RANK, MID * RANK), f32),
            pltpu.VMEM((LEAF, 8, PTS), f32), pltpu.VMEM((LANES, 8, 128), f32), pltpu.VMEM((LANES, 8, 128), f32),
            pltpu.VMEM((8, 128), f32), pltpu.VMEM((GROUPS, 8, 128), f32), pltpu.VMEM((8, 128), f32),
            pltpu.VMEM((LANES, 8, 128), f32),
            DMA((11,)), DMA((LANES,)), DMA((LANES,)), DMA((GROUPS,)), DMA((GROUPS,)), DMA((LANES,)), DMA((LANES,)),
            DMA((4,)), DMA((4,)),
        ],
        compiler_params=params(24, collective_id=0, has_side_effects=True),
        cost_estimate=cost(1000),
        name="first",
    )(lists, far2_list, coords, charges, basis, transfer1, transfer2, coupling2)
    acc = pl.pallas_call(
        far_kernel,
        out_shape=shape(LEAF, 64, PTS),
        in_specs=[SM] * 2 + [VM] * 10,
        out_specs=VM,
        scratch_shapes=[pltpu.VMEM((45, 128, 128), bf16)],
        compiler_params=params(24),
        cost_estimate=cost(1000),
        name="downward",
    )(far0_list, far1_list, pack, p1, p2, y2, coupling0, coupling1, transfer1, transfer2, basis, acc)
    return pl.pallas_call(
        rest_kernel,
        out_shape=shape(64, LEAF * PTS),
        in_specs=[SM] + [VM] * 4 + [ANY] * 5 + [VM],
        out_specs=VM,
        scratch_shapes=[
            pltpu.VMEM((LEAF + 1, 8, PTS), f32), pltpu.VMEM((3 * LEAF, 8, PTS), f32),
            pltpu.VMEM((3 * LEAF, PTS, 128), bf16), pltpu.VMEM((3 * LEAF, 128, PTS), bf16),
            pltpu.VMEM((LEAF + 1, 64, PTS), f32), pltpu.VMEM((2, 64, LEAF * PTS), f32), DMA((4,)),
        ],
        compiler_params=params(32),
        cost_estimate=cost(1000),
        name="rest",
    )(lists, pack, p1, p2, centres, feats, xs, x1, x2, x3, acc)


def solution(mesh):
    placed = (
        P(None, AXES),
        P(None, AXES),
        P(None, AXES),
        P(None, AXES),
        P(None, AXES),
        P(None, None, AXES),
        P(None, None, AXES),
        P(None, None, "grp"),
        P(AXES, None),
        P(AXES),
        P(AXES, None),
        P(AXES, None),
        P(),
    )
    return jax.shard_map(local, mesh=mesh, in_specs=placed, out_specs=P(None, AXES), check_vma=False)
```

time: 131 us -> 98.2 us (0.75)
  blocking collectives: 63.1 us -> 0 us
  Pallas kernels: 50.7 us -> 74.6 us
  local copies, waits for them, and re-layouts: 7.04 us -> 21.4 us
  starting transfers between devices: 9.14 us -> 1.28 us
    psum x1 -> x0, blocking collectives: 35.6 us -> none  [local(): tops = lax.all_gather(lax.psum(top, 'lane'), 'grp', axis=0, tiled=False)]
    all_gather x1 -> x0, blocking collectives: 27.5 us -> none  [local(): tops = lax.all_gather(lax.psum(top, 'lane'), 'grp', axis=0, tiled=False)]
    pallas_call x5 -> x4, Pallas kernels: 50.7 us -> 74.6 us  [the longest x1 47.1 us: local(): pl.pallas_call(first_kernel, out_shape=(shape(LEAF, 64, PTS), shape(18, 6...]
    unnamed x32 -> x58, local copies, waits for them, and re-layouts: 7.04 us -> 21.4 us
    ppermute x4 -> x1, starting transfers between devices: 9.14 us -> 1.28 us  [local(): lax.ppermute(charges, AXES, [(i, (i + 1) % DEVS) for i in range(1, DEVS,...]
  transfers between devices with their start and end apart: 4 -> 1, of which waited for: 0 -> 0; matrix products, arithmetic and copies ran while one was open for 1% -> 2% of each run, Pallas kernels for 32% -> 59%
where the time goes in v1:
time: 98.2 us; the launch traced here: 97.6 us
  Pallas kernels  74.6 us (76%)
  local copies, waits for them, and re-layouts  21.4 us (22%)
  starting transfers between devices  1.28 us (1%)
    pallas_call x1, Pallas kernels, local(): pl.pallas_call(first_kernel, out_shape=(shape(LEAF, 64, PTS), shape(18, 6...  47.1 us
    unnamed x58, local copies, waits for them, and re-layouts  21.4 us
    pallas_call x1, Pallas kernels, local(): pl.pallas_call(rest_kernel, out_shape=shape(64, LEAF * PTS), in_specs=[SM...  16.8 us
    pallas_call x1, Pallas kernels, local(): pl.pallas_call(far_kernel, out_shape=shape(LEAF, 64, PTS), in_specs=[SM]...  7.31 us
    pallas_call x1, Pallas kernels, local(): pl.pallas_call(list_kernel, out_shape=shape(LIST, dtype=jnp.int32), in_sp...  3.49 us
  transfers between devices with their start and end apart: 1, of which 0 were waited for; matrix products, arithmetic and copies ran while one was open for 2% of the time, Pallas kernels for 59%

profile of v1, /device:TPU:0, one launch (start us, length us, event | category | flops | bytes accessed | tf_op | source)
XLA Modules:
  0.0 97.6 jit_solution(4675790774724217361)
XLA Ops:
  0.0 1.3 %collective-permute-start = (f32[64,6144]{1,0:T(8,128)}, f32[64,6144]{1,0:T(8,128)}, u32[]{:S(2)}, u32[]{:S(2)}) collective-permute-start(f32[64,6144]{1,0:T(8,128)} %x_hbm.1), channel_id=1, source_target_pairs={{1,2},{3,4},{5,6},{7,8},{9,10},{11,12},{13,14},{15,16},{17,18},{19... | collective-permute-start | bytes 4718600 | tf_op jit(solution)/shard_map/ppermute | solution.py:485
  1.3 1.4 %copy.14.near_ref = s32[24,9]{1,0:T(8,128)} copy(s32[24,9]{0,1:T(8,128)} %param.21) | data formatting | bytes 1728 | tf_op args[8]
  2.7 3.5 %lists.1.list_ref = s32[512]{0:T(512)} custom-call(s32[24,9]{1,0:T(8,128)} %copy.14.near_ref, s32[24]{0:T(128)} %count_ref.1), custom_call_target="tpu_custom_call" | custom-call | flops 1000 | bytes 1000 | tf_op jit(solution)/shard_map/lists/pallas_call | solution.py:486
  6.2 0.8 copy.15.far2_ref
  6.9 1.4 %copy-done = f32[256,1536]{1,0:T(8,128)S(1)} copy-done((f32[256,1536]{1,0:T(8,128)S(1)}, f32[256,1536]{1,0:T(8,128)}, u32[]{:S(2)}) %copy-start) | copy-done | bytes 1572888
  8.3 1.0 %copy-done.7 = f32[64,1536]{1,0:T(8,128)S(1)} copy-done((f32[64,1536]{1,0:T(8,128)S(1)}, f32[64,1536]{1,0:T(8,128)}, u32[]{:S(2)}) %copy-start.7) | copy-done | bytes 393240
  9.3 1.4 %copy-done.9 = f32[64,6144]{1,0:T(8,128)S(1)} copy-done((f32[64,6144]{1,0:T(8,128)S(1)}, f32[64,6144]{1,0:T(8,128)}, u32[]{:S(2)}) %copy-start.9) | copy-done | bytes 1572888
  10.7 0.9 copy-done.17
  11.6 0.9 copy-done.21
  12.5 0.9 copy-done.22
  13.4 0.7 copy-done.23
  14.1 47.1 %first.1 = (f32[24,64,256]{2,1,0:T(8,128)S(1)}, f32[18,64,128]{2,1,0:T(8,128)S(1)}, f32[18,64,128]{2,1,0:T(8,128)S(1)}, f32[18,64,128]{2,1,0:T(8,128)S(1)}, f32[...) custom-call(s32[512]{0:T(512)S(1)} %copy-done.23, ...), custom_call_target="tpu_custom_call" | custom-call | flops 1000 | bytes 1000 | tf_op jit(solution)/shard_map/first/pallas_call | solution.py:490
  61.2 0.0 copy-start.3
  61.2 1.2 %copy-done.3 = bf16[25,256,128]{2,1,0:T(8,128)(2,1)} copy-done((bf16[25,256,128]{2,1,0:T(8,128)(2,1)}, bf16[25,256,128]{2,1,0:T(8,128)(2,1)S(1)}, u32[]{:S(2)}) %copy-start.3) | copy-done | bytes 1638424
  62.4 1.2 %copy-done.5 = bf16[25,128,256]{2,1,0:T(8,128)(2,1)} copy-done((bf16[25,128,256]{2,1,0:T(8,128)(2,1)}, bf16[25,128,256]{2,1,0:T(8,128)(2,1)S(1)}, u32[]{:S(2)}) %copy-start.5) | copy-done | bytes 1638424
  63.5 1.1 %copy-done.10 = f32[64,6144]{1,0:T(8,128)} copy-done((f32[64,6144]{1,0:T(8,128)}, f32[64,6144]{1,0:T(8,128)S(1)}, u32[]{:S(2)}) %copy-start.10) | copy-done | bytes 1572888
  64.7 1.2 %copy-done.12 = f32[64,6144]{1,0:T(8,128)} copy-done((f32[64,6144]{1,0:T(8,128)}, f32[64,6144]{1,0:T(8,128)S(1)}, u32[]{:S(2)}) %copy-start.12) | copy-done | bytes 1572888
  65.9 1.1 %copy-done.14 = f32[24,64,256]{2,1,0:T(8,128)} copy-done((f32[24,64,256]{2,1,0:T(8,128)}, f32[24,64,256]{2,1,0:T(8,128)S(1)}, u32[]{:S(2)}) %copy-start.14) | copy-done | bytes 1572888
  67.1 0.7 copy-done.19
  67.8 0.0 copy-done.25
  67.8 0.1 copy.16.far0_ref
  67.8 0.0 copy-done.26
  67.8 0.1 copy.17.far1_ref
  67.9 0.0 copy-done.1
  67.9 0.0 copy-done.18
  67.9 1.9 %copy-done.2 = f32[8,64,1536]{2,1,0:T(8,128)S(1)} copy-done((f32[8,64,1536]{2,1,0:T(8,128)S(1)}, f32[8,64,1536]{2,1,0:T(8,128)}, u32[]{:S(2)}) %copy-start.2) | copy-done | bytes 3145752
  69.8 1.0 %copy-done.8 = f32[64,1536]{1,0:T(8,128)S(1)} copy-done((f32[64,1536]{1,0:T(8,128)S(1)}, f32[64,1536]{1,0:T(8,128)}, u32[]{:S(2)}) %copy-start.8) | copy-done | bytes 393240
  70.8 1.4 %copy-done.15 = f32[24,64,256]{2,1,0:T(8,128)S(1)} copy-done((f32[24,64,256]{2,1,0:T(8,128)S(1)}, f32[24,64,256]{2,1,0:T(8,128)}, u32[]{:S(2)}) %copy-start.15) | copy-done | bytes 1572888
  72.2 1.0 %copy-done.16 = f32[4,64,384]{2,1,0:T(8,128)S(1)} copy-done((f32[4,64,384]{2,1,0:T(8,128)S(1)}, f32[4,64,384]{2,1,0:T(8,128)}, u32[]{:S(2)}) %copy-start.16) | copy-done | bytes 393240
  73.3 7.3 %downward.1.acc_in = f32[24,64,256]{2,1,0:T(8,128)S(1)} custom-call(s32[24,8]{1,0:T(8,128)S(1)} %copy.16.far0_ref, s32[6,4]{1,0:T(8,128)S(1)} %copy.17.far1_ref, f32[18,64,128]{2,1,0:T(8,128)S(1)} %get-tuple-element.15.p0_ref.own_ref, f32[18,64,128]{2,1,0:T(8,128)S(1)} %get-tuple-element.16.p1_ref, f32[18,64,128]{2,1,0:T(8,128)S(1)} %get-tuple-element.17.p2_ref, ...), custom_call_target="tpu_custom_call" | custom-call | flops 1000 | bytes 1000 | tf_op jit(solution)/shard_map/downward/pallas_call | solution.py:512
  80.6 0.0 collective-permute-done.x3_hbm
  80.6 16.8 %rest.1 = f32[64,6144]{1,0:T(8,128)} custom-call(s32[512]{0:T(512)S(1)} %copy-done.24, f32[18,64,128]{2,1,0:T(8,128)S(1)} %get-tuple-element.15.p0_ref.own_ref, f32[18,64,128]{2,1,0:T(8,128)S(1)} %get-tuple-element.16.p1_ref, f32[18,64,128]{2,1,0:T(8,128)S(1)} %get-tuple-element.17.p2_ref, f32[25,8,256]{2,1,0:T(8,128)S(1)} %copy-done.20, ...), custom_call_target="tpu_custom_call" | custom-call | flops 1000 | bytes 1000 | tf_op jit(solution)/shard_map/rest/pallas_call | solution.py:522
  (32 shorter events, 0.1 us)
Async XLA Ops:
  0.0 80.6 %collective-permute-start = (f32[64,6144]{1,0:T(8,128)}, f32[64,6144]{1,0:T(8,128)}, u32[]{:S(2)}, u32[]{:S(2)}) collective-permute-start(f32[64,6144]{1,0:T(8,128)} %x_hbm.1), channel_id=1, source_target_pairs={{1,2},{3,4},{5,6},{7,8},{9,10},{11,12},{13,14},{15,16},{17,18},{19... | collective-permute-start | bytes 4718600 | tf_op jit(solution)/shard_map/ppermute | solution.py:485
  6.9 1.4 %copy-start = (f32[256,1536]{1,0:T(8,128)S(1)}, f32[256,1536]{1,0:T(8,128)}, u32[]{:S(2)}) copy-start(f32[256,1536]{1,0:T(8,128)} %basis_ref.1) | copy-start | bytes 4718596
  8.3 1.0 %copy-start.7 = (f32[64,1536]{1,0:T(8,128)S(1)}, f32[64,1536]{1,0:T(8,128)}, u32[]{:S(2)}) copy-start(f32[64,1536]{1,0:T(8,128)} %t1_ref.1) | copy-start | bytes 1179652
  9.3 1.4 %copy-start.9 = (f32[64,6144]{1,0:T(8,128)S(1)}, f32[64,6144]{1,0:T(8,128)}, u32[]{:S(2)}) copy-start(f32[64,6144]{1,0:T(8,128)} %x_hbm.1) | copy-start | bytes 4718596
  10.7 0.9 copy-start.17
  11.6 0.9 copy-start.21
  12.5 0.9 copy-start.22
  13.4 0.7 copy-start.23
  14.1 53.7 %copy-start.25 = (s32[24,8]{0,1:T(8,128)S(1)}, s32[24,8]{0,1:T(8,128)}, u32[]{:S(2)}) copy-start(s32[24,8]{0,1:T(8,128)} %param.23) | copy-start | bytes 2308
  14.1 53.7 %copy-start.26 = (s32[6,4]{0,1:T(4,128)S(1)}, s32[6,4]{0,1:T(4,128)}, u32[]{:S(2)}) copy-start(s32[6,4]{0,1:T(4,128)} %param.24) | copy-start | bytes 292
  14.1 53.8 %copy-start.1 = (f32[256,1536]{1,0:T(8,128)S(1)}, f32[256,1536]{1,0:T(8,128)}, u32[]{:S(2)}) copy-start(f32[256,1536]{1,0:T(8,128)} %basis_ref.1) | copy-start | bytes 4718596
  14.1 53.8 %copy-start.18 = (f32[64,384]{1,0:T(8,128)S(1)}, f32[64,384]{1,0:T(8,128)}, u32[]{:S(2)}) copy-start(f32[64,384]{1,0:T(8,128)} %t2_ref.1) | copy-start | bytes 294916
  61.2 1.2 %copy-start.3 = (bf16[25,256,128]{2,1,0:T(8,128)(2,1)}, bf16[25,256,128]{2,1,0:T(8,128)(2,1)S(1)}, u32[]{:S(2)}) copy-start(bf16[25,256,128]{2,1,0:T(8,128)(2,1)S(1)} %get-tuple-element.19.own_feats) | copy-start | bytes 4915204
  62.4 1.2 %copy-start.5 = (bf16[25,128,256]{2,1,0:T(8,128)(2,1)}, bf16[25,128,256]{2,1,0:T(8,128)(2,1)S(1)}, u32[]{:S(2)}) copy-start(bf16[25,128,256]{2,1,0:T(8,128)(2,1)S(1)} %get-tuple-element.20.own_xs) | copy-start | bytes 4915204
  63.5 1.1 %copy-start.10 = (f32[64,6144]{1,0:T(8,128)}, f32[64,6144]{1,0:T(8,128)S(1)}, u32[]{:S(2)}) copy-start(f32[64,6144]{1,0:T(8,128)S(1)} %get-tuple-element.21.x1_hbm) | copy-start | bytes 4718596
  64.7 1.2 %copy-start.12 = (f32[64,6144]{1,0:T(8,128)}, f32[64,6144]{1,0:T(8,128)S(1)}, u32[]{:S(2)}) copy-start(f32[64,6144]{1,0:T(8,128)S(1)} %get-tuple-element.22.x2_hbm) | copy-start | bytes 4718596
  65.9 1.2 %copy-start.14 = (f32[24,64,256]{2,1,0:T(8,128)}, f32[24,64,256]{2,1,0:T(8,128)S(1)}, u32[]{:S(2)}) copy-start(f32[24,64,256]{2,1,0:T(8,128)S(1)} %get-tuple-element.24.acc_in) | copy-start | bytes 4718596
  67.0 0.7 copy-start.19
  67.9 1.9 %copy-start.2 = (f32[8,64,1536]{2,1,0:T(8,128)S(1)}, f32[8,64,1536]{2,1,0:T(8,128)}, u32[]{:S(2)}) copy-start(f32[8,64,1536]{2,1,0:T(8,128)} %c0_ref.1) | copy-start | bytes 9437188
  69.8 1.0 %copy-start.8 = (f32[64,1536]{1,0:T(8,128)S(1)}, f32[64,1536]{1,0:T(8,128)}, u32[]{:S(2)}) copy-start(f32[64,1536]{1,0:T(8,128)} %t1_ref.1) | copy-start | bytes 1179652
  70.8 1.4 %copy-start.15 = (f32[24,64,256]{2,1,0:T(8,128)S(1)}, f32[24,64,256]{2,1,0:T(8,128)}, u32[]{:S(2)}) copy-start(f32[24,64,256]{2,1,0:T(8,128)} %copy-done.14) | copy-start | bytes 4718596
  72.2 1.0 %copy-start.16 = (f32[4,64,384]{2,1,0:T(8,128)S(1)}, f32[4,64,384]{2,1,0:T(8,128)}, u32[]{:S(2)}) copy-start(f32[4,64,384]{2,1,0:T(8,128)} %c1_ref.1) | copy-start | bytes 1179652
  73.2 7.4 %copy-start.4 = (bf16[25,256,128]{2,1,0:T(8,128)(2,1)S(1)}, bf16[25,256,128]{2,1,0:T(8,128)(2,1)}, u32[]{:S(2)}) copy-start(bf16[25,256,128]{2,1,0:T(8,128)(2,1)} %copy-done.3) | copy-start | bytes 4915204
  73.2 7.4 %copy-start.6 = (bf16[25,128,256]{2,1,0:T(8,128)(2,1)S(1)}, bf16[25,128,256]{2,1,0:T(8,128)(2,1)}, u32[]{:S(2)}) copy-start(bf16[25,128,256]{2,1,0:T(8,128)(2,1)} %copy-done.5) | copy-start | bytes 4915204
  73.2 7.4 %copy-start.11 = (f32[64,6144]{1,0:T(8,128)S(1)}, f32[64,6144]{1,0:T(8,128)}, u32[]{:S(2)}) copy-start(f32[64,6144]{1,0:T(8,128)} %copy-done.10) | copy-start | bytes 4718596
  73.2 7.4 %copy-start.13 = (f32[64,6144]{1,0:T(8,128)S(1)}, f32[64,6144]{1,0:T(8,128)}, u32[]{:S(2)}) copy-start(f32[64,6144]{1,0:T(8,128)} %copy-done.12) | copy-start | bytes 4718596
  73.2 7.4 %copy-start.20 = (f32[25,8,256]{2,1,0:T(8,128)S(1)}, f32[25,8,256]{2,1,0:T(8,128)}, u32[]{:S(2)}) copy-start(f32[25,8,256]{2,1,0:T(8,128)} %copy-done.19) | copy-start | bytes 614404
  73.2 7.4 %copy-start.24 = (s32[512]{0:T(512)S(1)}, s32[512]{0:T(512)}, u32[]{:S(2)}) copy-start(s32[512]{0:T(512)} %lists.1.list_ref) | copy-start | bytes 6148

commit v2 on v1

v2 whole, which is shorter than its diff:
```python
import math

import jax
import jax.numpy as jnp
from jax import lax
from jax.experimental import pallas as pl
from jax.experimental.pallas import tpu as pltpu
from jax.sharding import PartitionSpec as P

AXES = ("grp", "lane")
LANES = 8
DEVS = 128
LEAF = 24
MID = 6
PTS = 256
RANK = 64
NEAR = 9
FAR0 = 8
FAR1 = 4
FAR2 = 4
UNROLL = 18
SLOTS = 5
REST_ROW = 8
COUNT_ROW = 9
CHUNK = 512
GROUPS = 16
MESH = pl.DeviceIdType.MESH
inv_four_pi = 1.0 / (4.0 * math.pi)
smooth_sq = 5e-05
bf16 = jnp.bfloat16
f32 = jnp.float32
NT = (((1,), (1,)), ((), ()))


def dot(a, b, dims=(((1,), (0,)), ((), ()))):
    return lax.dot_general(a, b, dims, preferred_element_type=f32)


def split(a):
    high = a.astype(bf16)
    return high, (a - high.astype(f32)).astype(bf16)


def lanes_low(shape):
    return lax.broadcasted_iota(jnp.int32, shape, len(shape) - 1) < RANK


def swap_halves(a):
    return pltpu.roll(a, RANK, 1)


def halves(tile):
    low = lanes_low(tile.shape)
    return jnp.where(low, tile, 0.0), jnp.where(low, 0.0, tile)


def place_of():
    return lax.axis_index("grp") * LANES + lax.axis_index("lane")


def source_of(entry, place, width):
    even = lax.rem(place, 2) == 0
    rel = entry - place * width
    rel = jnp.where(rel < -width, rel + DEVS * width, jnp.where(rel >= 2 * width, rel - DEVS * width, rel))
    low_off = jnp.where(even, 3 * width, 2 * width)
    high_off = jnp.where(even, 0, width)
    source = rel + jnp.where(rel < 0, low_off, jnp.where(rel >= width, high_off, 0))
    return jnp.minimum(jnp.maximum(source, 0), 3 * width - 1)


def stacked_split(rows_a, rows_b):
    ah, al = split(rows_a)
    bh, bl = split(rows_b)
    return jnp.concatenate([ah, bh, al, bl], axis=0)


def wide_split(a):
    h, l = split(a)
    return jnp.concatenate([h, l], axis=1)


def fold(out):
    s = out[:, :128] + out[:, 128:]
    return s[0:64] + s[128:192], s[64:128] + s[192:256]


def transposed(rows_a, rows_b, weights):
    lhs = stacked_split(rows_a, rows_b)
    wh, wl = split(weights)
    r = dot(lhs, wh, NT)
    r2 = dot(lhs[:128], wl, NT)
    return r[0:64] + r[128:192] + r2[0:64], r[64:128] + r[192:256] + r2[64:128]


def list_kernel(near_ref, count_ref, out_ref):
    place = place_of()
    source = source_of(near_ref[...], place, LEAF)
    count = count_ref[...]
    leaf = lax.broadcasted_iota(jnp.int32, (1, LEAF), 1)
    own_at = jnp.zeros((1, LEAF), jnp.int32)
    rest_at = jnp.zeros((1, LEAF), jnp.int32)
    own = [jnp.full((1, LEAF), LEAF, jnp.int32) for _ in range(SLOTS - 1)]
    places = []
    for k in range(1, NEAR):
        src = source[k:k + 1]
        live = count > k
        here = jnp.logical_and(jnp.logical_and(src < LEAF, live), own_at < SLOTS - 1)
        for s in range(SLOTS - 1):
            own[s] = jnp.where(jnp.logical_and(here, own_at == s), src, own[s])
        own_at = own_at + jnp.where(here, 1, 0)
        rest = jnp.logical_and(live, jnp.logical_not(here))
        places.append((rest, rest_at))
        rest_at = rest_at + jnp.where(rest, 1, 0)
    row = lax.broadcasted_iota(jnp.int32, (LEAF, LEAF), 0)
    col = lax.broadcasted_iota(jnp.int32, (LEAF, LEAF), 1)
    before = jnp.where(row < col, 1.0, 0.0).astype(bf16)
    counts = jnp.broadcast_to(rest_at.astype(f32), (16, LEAF)).astype(bf16)
    base = dot(counts, before)[0:1]
    at = [jnp.where(rest, base + pos.astype(f32), -1.0) for rest, pos in places]
    values = jnp.concatenate(at + [source[k:k + 1].astype(f32) for k in range(1, NEAR)], axis=0).astype(bf16)
    columns = dot(jnp.where(row == col, 1.0, 0.0).astype(bf16), values, NT)
    lanes = lax.broadcasted_iota(jnp.int32, (LEAF, PTS), 1).astype(f32)
    word = lax.broadcasted_iota(jnp.int32, (LEAF, 1), 0).astype(f32) * 128.0
    flat = jnp.zeros((LEAF, PTS), f32)
    for k in range(NEAR - 1):
        flat = flat + jnp.where(columns[:, k:k + 1] == lanes, word + columns[:, NEAR - 1 + k:NEAR + k], 0.0)
    flat = jnp.sum(flat, axis=0, keepdims=True)
    total = jnp.sum(rest_at.astype(f32), axis=1, keepdims=True)
    flat = jnp.where(lanes[0:1] < total, flat, LEAF * 128.0)
    out_ref[...] = jnp.zeros((16, PTS), jnp.int32)
    out_ref[0:1, 0:LEAF] = leaf
    for s in range(SLOTS - 1):
        out_ref[s + 1:s + 2, 0:LEAF] = own[s]
    out_ref[REST_ROW:REST_ROW + 1, :] = flat.astype(jnp.int32)
    out_ref[COUNT_ROW:COUNT_ROW + 1, :] = jnp.broadcast_to(total, (1, PTS)).astype(jnp.int32)


def upward(coords_ref, x_ref, basis_ref, t1_ref, t2_ref, pack_ref):
    tiles = []
    for t in range(LEAF // 2):
        xa = x_ref[:, t * 512:t * 512 + 256]
        xb = x_ref[:, t * 512 + 256:t * 512 + 512]
        ra, rb = fold(dot(stacked_split(xa, xb), wide_split(basis_ref[:, t * 128:t * 128 + 128])))
        q = jnp.where(lanes_low(ra.shape), ra, rb)
        pack_ref[t] = q
        tiles.append(q)
    mids = []
    parts = []
    for m in range(MID):
        a0, b0 = halves(tiles[2 * m])
        a1, b1 = halves(tiles[2 * m + 1])
        e0 = t1_ref[:, m * 256:m * 256 + 128]
        e1 = t1_ref[:, m * 256 + 128:m * 256 + 256]
        lhs = stacked_split(jnp.concatenate([a0, a1], axis=1), jnp.concatenate([b0, b1], axis=1))
        parts.append(fold(dot(lhs, wide_split(jnp.concatenate([e0, e0, e1, e1], axis=0)))))
    for t in range(MID // 2):
        (top0, bot0), (top1, bot1) = parts[2 * t], parts[2 * t + 1]
        low = lanes_low(top0.shape)
        mid = jnp.where(low, top0, bot1) + swap_halves(jnp.where(low, top1, bot0))
        pack_ref[LEAF // 2 + t] = mid
        mids.append(mid)
    both = [halves(m) for m in mids]
    weights = [t2_ref[:, t * 128:t * 128 + 128] for t in range(MID // 2)]
    lhs = stacked_split(
        jnp.concatenate([b[0] for b in both], axis=1), jnp.concatenate([b[1] for b in both], axis=1)
    )
    top, bot = fold(dot(lhs, wide_split(jnp.concatenate([w for w in weights for _ in range(2)], axis=0))))
    for i in range(2 * LEAF):
        for c in range(3):
            pack_ref[15 + c, i:i + 1, :] = coords_ref[c:c + 1, i * 128:i * 128 + 128]
    zero = jnp.zeros((16, 128), f32)
    for c in range(3):
        pack_ref[15 + c, 48:64, :] = zero
    s = jnp.where(lanes_low(top.shape), top, bot)
    return s + swap_halves(s)


def leaf_rows(pack_ref, leaf):
    row = lax.broadcasted_iota(jnp.int32, (8, PTS), 0)
    out = jnp.zeros((8, PTS), f32)
    for c in range(3):
        line = jnp.concatenate(
            [pack_ref[15 + c, 2 * leaf:2 * leaf + 1, :], pack_ref[15 + c, 2 * leaf + 1:2 * leaf + 2, :]], axis=1
        )
        out = jnp.where(row == c, line, out)
    return out


def pieces(a):
    h = a.astype(bf16).astype(f32)
    r = a - h
    m = r.astype(bf16).astype(f32)
    return h, m, r - m


def identity():
    return jnp.where(
        lax.broadcasted_iota(jnp.int32, (PTS, PTS), 0) == lax.broadcasted_iota(jnp.int32, (PTS, PTS), 1), 1.0, 0.0
    ).astype(bf16)


def prepare(pack_ref, x_ref, leaf, at, eye, centres, feats, xs):
    row = lax.broadcasted_iota(jnp.int32, (8, PTS), 0)
    source = leaf_rows(pack_ref, leaf)
    centre = jnp.broadcast_to(jnp.sum(source, axis=1, keepdims=True) * (1.0 / PTS), (8, PTS))
    centres[at] = centre
    d = source - centre
    sq = jnp.sum(d * d, axis=0, keepdims=True) + smooth_sq
    h, m, l = pieces(jnp.where(row < 3, -2.0 * d, jnp.where(row == 3, 1.0, jnp.where(row == 4, sq, 0.0))))
    rows = jnp.concatenate([h, m, h, l, m, h, jnp.zeros((80, PTS), f32)], axis=0).astype(bf16)
    feats[at] = dot(eye, rows, NT).astype(bf16)
    xh, xl = split(x_ref[:, leaf * PTS:leaf * PTS + PTS] * inv_four_pi)
    xs[at] = jnp.concatenate([xh, xl], axis=0)


def pairs(ls, js, targets, centres, feats, xs, acc):
    unit = jnp.where(lax.broadcasted_iota(jnp.int32, (8, PTS), 0) == 4, 1.0, 0.0)
    row = lax.broadcasted_iota(jnp.int32, (8, PTS), 0)
    dist = []
    for l, j in zip(ls, js):
        d = targets[l] - centres[j]
        sq = jnp.sum(d * d, axis=0, keepdims=True)
        h, m, low = pieces(jnp.where(row == 3, sq, d + unit))
        rows = jnp.concatenate([h, h, m, h, m, low], axis=0).astype(bf16)
        dist.append(dot(feats[j][:, :48], rows))
    for l, j, d2 in zip(ls, js, dist):
        kh, kl = split(lax.rsqrt(d2))
        x = xs[j]
        r = dot(x, kh) + dot(x, kl)
        acc[l] += r[:64] + r[64:]


def place_tile(tile, low_ref, high_ref, at):
    other = swap_halves(tile)
    low = lanes_low(tile.shape)
    for i, (here, there) in enumerate(((tile, other), (other, tile))):
        h, l = split(jnp.where(low, here, 0.0))
        low_ref[at + i] = jnp.concatenate([h, l], axis=0)
        h, l = split(jnp.where(low, 0.0, there))
        high_ref[at + i] = jnp.concatenate([h, l], axis=0)


def coupled(sources, weights, low_ref, high_ref):
    lhs = jnp.concatenate(
        [
            jnp.concatenate([low_ref[row[f]] + high_ref[row[f + 1]] for f in range(0, len(row), 2)], axis=1)
            for row in sources
        ],
        axis=0,
    )
    out = dot(lhs, wide_split(jnp.concatenate(weights, axis=0)))
    s = out[:, :128] + out[:, 128:]
    even, odd = s[0:64] + s[64:128], s[128:192] + s[192:256]
    return jnp.where(lanes_low(even.shape), even, odd)


def top_coupled(picks, c2_ref):
    tiles = []
    for f in range(0, FAR2, 2):
        a = jnp.concatenate([picks[f], swap_halves(picks[f])], axis=0)
        b = jnp.concatenate([swap_halves(picks[f + 1]), picks[f + 1]], axis=0)
        tiles.append(jnp.where(lanes_low(a.shape), a, b))
    th, tl = split(jnp.concatenate(tiles, axis=1))
    w = jnp.concatenate([c2_ref[f] for f in range(FAR2)], axis=0)
    wh, wl = split(jnp.concatenate([w, w], axis=1))
    y2 = dot(th, wh) + dot(tl, wh) + dot(th, wl)
    return jnp.where(lanes_low((32, 128)), y2[:32], y2[32:])


def main_kernel(
    list_ref, far0_ref, far1_ref, far2_ref, coords_hbm, x_hbm, basis_hbm, t1_hbm, t2_hbm, c0_hbm, c1_hbm, c2_hbm,
    acc_out, pack_out, p2_ref, x2_ref, centres_out, feats_out, xs_out,
    coords, x, x1, basis, t1, t2, c0, c1, c2, pack, p1, p2, acc, targets, centres, feats, xs,
    part, parts, y2_part, y2_parts, y1, q_low, q_high, m_low, m_high,
    load_sem, part_send, part_recv, y2_send, y2_recv, pack_send, pack_recv, e_send, e_recv, n_send, n_recv, out_sem,
):
    group = lax.axis_index("grp")
    lane = lax.axis_index("lane")
    place = group * LANES + lane
    even = lax.rem(lane, 2) == 0
    partner = (group, lane + 1 - 2 * lax.rem(lane, 2))
    beyond = lax.rem(place + jnp.where(even, DEVS - 1, 1), DEVS)
    beyond = (beyond // LANES, lax.rem(beyond, LANES))

    barrier = pltpu.get_barrier_semaphore()
    for d in range(1, LANES):
        pl.semaphore_signal(barrier, inc=1, device_id=(group, lax.rem(lane + d, LANES)), device_id_type=MESH)
    for d in range(1, GROUPS):
        pl.semaphore_signal(barrier, inc=1, device_id=(lax.rem(group + d, GROUPS), lane), device_id_type=MESH)
    pl.semaphore_signal(barrier, inc=1, device_id=beyond, device_id_type=MESH)

    loads = [
        pltpu.make_async_copy(src, dst, load_sem.at[i])
        for i, (src, dst) in enumerate(
            [(x_hbm.at[:, c * 1536:c * 1536 + 1536], x.at[:, c * 1536:c * 1536 + 1536]) for c in range(4)]
            + [(basis_hbm.at[r * 64:r * 64 + 64], basis.at[r * 64:r * 64 + 64]) for r in range(4)]
            + [(t1_hbm, t1), (t2_hbm, t2), (coords_hbm, coords)]
            + [(c0_hbm.at[r * 2:r * 2 + 2], c0.at[r * 2:r * 2 + 2]) for r in range(4)]
            + [(c1_hbm, c1), (c2_hbm, c2)]
        )
    ]
    for c in loads:
        c.start()
    for c in loads[:11]:
        c.wait()
    top = upward(coords, x, basis, t1, t2, pack)
    part[...] = jnp.where(lanes_low((32, 128)), top[:32], top[32:])
    pl.semaphore_wait(barrier, LANES + GROUPS - 1)

    def part_copy(d):
        peer = lax.rem(group + d, GROUPS)
        return (
            pltpu.make_async_remote_copy(
                part, parts.at[group], part_send.at[d], part_recv.at[group], (peer, lane), MESH
            ),
            pltpu.make_async_remote_copy(
                part, parts.at[peer], part_send.at[d], part_recv.at[peer], (peer, lane), MESH
            ),
        )

    def y2_copy(d):
        peer = lax.rem(lane + d, LANES)
        return (
            pltpu.make_async_remote_copy(
                y2_part, y2_parts.at[lane], y2_send.at[d], y2_recv.at[lane], (group, peer), MESH
            ),
            pltpu.make_async_remote_copy(
                y2_part, y2_parts.at[peer], y2_send.at[d], y2_recv.at[peer], (group, peer), MESH
            ),
        )

    def chunk(i, src, dst, send, recv, device):
        at = (slice(None), pl.ds(pl.multiple_of(i * CHUNK, CHUNK), CHUNK))
        return pltpu.make_async_remote_copy(src.at[at], dst.at[at], send.at[i], recv.at[i], device, MESH)

    def near_chunks(i):
        return chunk(i, x, x2_ref, n_send, n_recv, beyond), chunk(i, x, x1, e_send, e_recv, partner)

    for d in range(1, GROUPS):
        part_copy(d)[0].start()
    packs = [
        pltpu.make_async_remote_copy(pack, p2, pack_send.at[0], pack_recv.at[0], beyond, MESH),
        pltpu.make_async_remote_copy(pack, p1, pack_send.at[1], pack_recv.at[1], partner, MESH),
    ]
    for c in packs:
        c.start()
    for c in near_chunks(0):
        c.start()

    eye = identity()
    for leaf in range(LEAF):
        targets[leaf] = leaf_rows(pack, leaf)
        prepare(pack, x, leaf, leaf, eye, centres, feats, xs)
        acc[leaf] = jnp.zeros((64, PTS), f32)
    centres[2 * LEAF] = jnp.zeros((8, PTS), f32)
    feats[2 * LEAF] = feats[0]
    xs[2 * LEAF] = jnp.zeros((128, PTS), bf16)

    def leaves(i):
        ls = [2 * i + u for u in range(2) for s in range(SLOTS)]
        js = [list_ref[s, 2 * i + u] for u in range(2) for s in range(SLOTS)]
        pairs(ls, [jnp.where(j == LEAF, 2 * LEAF, j) for j in js], targets, centres, feats, xs, acc)

    def step(i, _):
        for c in near_chunks(i + 1):
            c.start()
        leaves(i)
        return 0

    lax.fori_loop(0, 4, step, 0)

    for c in loads[11:]:
        c.wait()
    for d in range(1, GROUPS):
        part_copy(d)[1].wait_recv()
    parts[group] = part[...]
    mine = top_coupled([parts[far2_ref[f, group]] for f in range(FAR2)], c2)
    y2_part[...] = mine
    y2_parts[lane] = mine
    for d in range(1, LANES):
        y2_copy(d)[0].start()

    lax.fori_loop(4, LEAF // 2 - 1, step, 0)
    leaves(LEAF // 2 - 1)

    for c in packs:
        c.wait()
    for b, p in enumerate((pack, p1, p2)):
        for t in range(LEAF // 2):
            place_tile(p[t], q_low, q_high, LEAF * b + 2 * t)
        for t in range(MID // 2):
            place_tile(p[LEAF // 2 + t], m_low, m_high, MID * b + 2 * t)
    for d in range(1, LANES):
        y2_copy(d)[1].wait_recv()
    y2 = y2_parts[0]
    for r in range(1, LANES):
        y2 = y2 + y2_parts[r]
    other = swap_halves(y2)
    low = lanes_low(y2.shape)
    y2 = jnp.concatenate([jnp.where(low, y2, other), jnp.where(low, other, y2)], axis=0)

    for t in range(MID // 2):
        at = slice(t * 128, t * 128 + 128)
        y = coupled(
            [[source_of(far1_ref[f, 2 * t + i], place, MID) for f in range(FAR1)] for i in range(2)],
            [c1[f, :, at] for f in range(FAR1)], m_low, m_high,
        )
        w = t2[:, at]
        one, two = transposed(*halves(y2), jnp.concatenate([w, w], axis=0))
        y = y + jnp.where(lanes_low(y.shape), one, two)
        other = swap_halves(y)
        low = lanes_low(y.shape)
        y1[2 * t] = jnp.where(low, y, other)
        y1[2 * t + 1] = jnp.where(low, other, y)

    def down(m, _):
        for u in range(2):
            t = 2 * m + u
            at = pl.ds(pl.multiple_of(t * 128, 128), 128)
            y = coupled(
                [[source_of(far0_ref[f, 2 * t + i], place, LEAF) for f in range(FAR0)] for i in range(2)],
                [c0[f, :, at] for f in range(FAR0)], q_low, q_high,
            )
            w = t1[:, at]
            one, two = transposed(*halves(y1[m]), jnp.concatenate([w, w], axis=0))
            y = y + jnp.where(lanes_low(y.shape), one, two)
            one, two = transposed(*halves(y), basis[:, at])
            acc[2 * t] += one
            acc[2 * t + 1] += two
        return 0

    lax.fori_loop(0, MID, down, 0)

    def arrived(i, _):
        chunk(i, x, x1, e_send, e_recv, partner).wait()
        return 0

    lax.fori_loop(0, LEAF // 2, arrived, 0)
    for leaf in range(LEAF):
        prepare(p1, x1, leaf, LEAF + leaf, eye, centres, feats, xs)
    outs = [
        pltpu.make_async_copy(src, dst, out_sem.at[i])
        for i, (src, dst) in enumerate(
            [
                (acc, acc_out), (pack, pack_out), (p2, p2_ref), (centres.at[0:48], centres_out),
                (feats.at[0:24], feats_out.at[0:24]), (feats.at[24:48], feats_out.at[24:48]),
                (xs.at[0:24], xs_out.at[0:24]), (xs.at[24:48], xs_out.at[24:48]),
            ]
        )
    ]
    for c in outs:
        c.start()
    for d in range(1, GROUPS):
        part_copy(d)[0].wait_send()
    for d in range(1, LANES):
        y2_copy(d)[0].wait_send()

    def sent(i, _):
        chunk(i, x, x2_ref, n_send, n_recv, beyond).wait()
        return 0

    lax.fori_loop(0, LEAF // 2, sent, 0)
    for c in outs:
        c.wait()


def rest_kernel(
    list_ref, own_hbm, p2_hbm, x2_hbm, acc_hbm, centres_hbm, feats_hbm, xs_hbm, out_ref,
    own, p2, targets, centres, feats, xs, acc, x, sem,
):
    moves = [
        pltpu.make_async_copy(src, dst, sem.at[i])
        for i, (src, dst) in enumerate(
            [(own_hbm, own), (p2_hbm, p2)]
            + [(x2_hbm.at[:, c * 1536:c * 1536 + 1536], x.at[:, c * 1536:c * 1536 + 1536]) for c in range(4)]
            + [
                (acc_hbm, acc.at[0:24]), (centres_hbm, centres.at[0:48]),
                (feats_hbm.at[0:24], feats.at[0:24]), (feats_hbm.at[24:48], feats.at[24:48]),
                (xs_hbm.at[0:24], xs.at[0:24]), (xs_hbm.at[24:48], xs.at[24:48]),
            ]
        )
    ]
    for c in moves:
        c.start()
    targets[LEAF] = jnp.zeros((8, PTS), f32)
    acc[LEAF] = jnp.zeros((64, PTS), f32)
    eye = identity()
    for c in moves[:6]:
        c.wait()
    for leaf in range(LEAF):
        targets[leaf] = leaf_rows(own, leaf)
        prepare(p2, x, leaf, 2 * LEAF + leaf, eye, centres, feats, xs)
    for c in moves[6:]:
        c.wait()

    @pl.loop(0, (list_ref[COUNT_ROW, 0] + (UNROLL - 1)) // UNROLL)
    def _(i):
        words = [list_ref[REST_ROW, i * UNROLL + u] for u in range(UNROLL)]
        pairs(
            [lax.shift_right_logical(w, 7) for w in words], [w & 127 for w in words], targets, centres, feats, xs, acc
        )

    for leaf in range(LEAF):
        out_ref[:, leaf * PTS:leaf * PTS + PTS] = acc[leaf]


VM = pl.BlockSpec(memory_space=pltpu.VMEM)
SM = pl.BlockSpec(memory_space=pltpu.SMEM)
ANY = pl.BlockSpec(memory_space=pl.ANY)
DMA = pltpu.SemaphoreType.DMA


def params(mib, **more):
    return pltpu.CompilerParams(vmem_limit_bytes=mib << 20, **more)


def cost(size):
    return pl.CostEstimate(flops=size, bytes_accessed=1000, transcendentals=0)


def shape(*dims, dtype=f32):
    return jax.ShapeDtypeStruct(dims, dtype)


def local(
    coords, charges, basis, transfer1, transfer2, coupling0, coupling1, coupling2, near_list, near_count, far0_list,
    far1_list, far2_list,
):
    lists = pl.pallas_call(
        list_kernel, out_shape=shape(16, PTS, dtype=jnp.int32), in_specs=[VM, VM], out_specs=VM,
        compiler_params=params(56), cost_estimate=cost(1000), name="lists",
    )(near_list.T, near_count.reshape(1, LEAF))
    wide = LEAF * PTS
    acc, pack, p2, x2, centres, feats, xs = pl.pallas_call(
        main_kernel,
        out_shape=(
            shape(LEAF, 64, PTS), shape(18, 64, 128), shape(18, 64, 128), shape(64, wide), shape(2 * LEAF, 8, PTS),
            shape(2 * LEAF, PTS, 128, dtype=bf16), shape(2 * LEAF, 128, PTS, dtype=bf16),
        ),
        in_specs=[SM] * 4 + [ANY] * 8,
        out_specs=(ANY,) * 7,
        scratch_shapes=[
            pltpu.VMEM((3, wide), f32), pltpu.VMEM((64, wide), f32), pltpu.VMEM((64, wide), f32),
            pltpu.VMEM((PTS, LEAF * RANK), f32), pltpu.VMEM((RANK, LEAF * RANK), f32),
            pltpu.VMEM((RANK, MID * RANK), f32), pltpu.VMEM((FAR0, RANK, LEAF * RANK), f32),
            pltpu.VMEM((FAR1, RANK, MID * RANK), f32), pltpu.VMEM((FAR2, RANK, RANK), f32),
            pltpu.VMEM((18, 64, 128), f32), pltpu.VMEM((18, 64, 128), f32), pltpu.VMEM((18, 64, 128), f32),
            pltpu.VMEM((LEAF, 64, PTS), f32), pltpu.VMEM((LEAF, 8, PTS), f32),
            pltpu.VMEM((2 * LEAF + 1, 8, PTS), f32), pltpu.VMEM((2 * LEAF + 1, PTS, 128), bf16),
            pltpu.VMEM((2 * LEAF + 1, 128, PTS), bf16),
            pltpu.VMEM((32, 128), f32), pltpu.VMEM((GROUPS, 32, 128), f32), pltpu.VMEM((32, 128), f32),
            pltpu.VMEM((LANES, 32, 128), f32), pltpu.VMEM((MID, 64, 128), f32),
            pltpu.VMEM((3 * LEAF, 128, 128), bf16), pltpu.VMEM((3 * LEAF, 128, 128), bf16),
            pltpu.VMEM((3 * MID, 128, 128), bf16), pltpu.VMEM((3 * MID, 128, 128), bf16),
            DMA((17,)), DMA((GROUPS,)), DMA((GROUPS,)), DMA((LANES,)), DMA((LANES,)), DMA((2,)), DMA((2,)),
            DMA((LEAF // 2,)), DMA((LEAF // 2,)), DMA((LEAF // 2,)), DMA((LEAF // 2,)), DMA((8,)),
        ],
        compiler_params=params(56, collective_id=0, has_side_effects=True),
        cost_estimate=cost(1000),
        name="main",
    )(
        lists, far0_list.T, far1_list.T, far2_list.T, coords, charges, basis, transfer1, transfer2, coupling0,
        coupling1, coupling2,
    )
    return pl.pallas_call(
        rest_kernel,
        out_shape=shape(64, wide),
        in_specs=[SM] + [ANY] * 7,
        out_specs=VM,
        scratch_shapes=[
            pltpu.VMEM((18, 64, 128), f32), pltpu.VMEM((18, 64, 128), f32), pltpu.VMEM((LEAF + 1, 8, PTS), f32),
            pltpu.VMEM((3 * LEAF, 8, PTS), f32), pltpu.VMEM((3 * LEAF, PTS, 128), bf16),
            pltpu.VMEM((3 * LEAF, 128, PTS), bf16), pltpu.VMEM((LEAF + 1, 64, PTS), f32), pltpu.VMEM((64, wide), f32),
            DMA((12,)),
        ],
        compiler_params=params(56),
        cost_estimate=cost(1000),
        name="rest",
    )(lists, pack, p2, x2, acc, centres, feats, xs)


def solution(mesh):
    placed = (
        P(None, AXES),
        P(None, AXES),
        P(None, AXES),
        P(None, AXES),
        P(None, AXES),
        P(None, None, AXES),
        P(None, None, AXES),
        P(None, None, "grp"),
        P(AXES, None),
        P(AXES),
        P(AXES, None),
        P(AXES, None),
        P(),
    )
    return jax.shard_map(local, mesh=mesh, in_specs=placed, out_specs=P(None, AXES), check_vma=False)
```

time: 98.2 us -> 69.5 us (0.71)
  local copies, waits for them, and re-layouts: 21.4 us -> 0 us
  Pallas kernels: 74.6 us -> 69.2 us
  starting transfers between devices: 1.28 us -> 0 us
    unnamed x58 -> x0, local copies, waits for them, and re-layouts: 21.4 us -> none
    pallas_call x4 -> x3, Pallas kernels: 74.6 us -> 69.2 us  [the longest x1 49.2 us: local(): pl.pallas_call(main_kernel, out_shape=(shape(LEAF, 64, PTS), shape(18, 64...]
    ppermute x1 -> x0, starting transfers between devices: 1.28 us -> none  [local(): lax.ppermute(charges, AXES, [(i, (i + 1) % DEVS) for i in range(1, DEVS,...]
  transfers between devices with their start and end apart: 1 -> 0, of which waited for: 0 -> 0; matrix products, arithmetic and copies ran while one was open for 2% -> 0% of each run, Pallas kernels for 59% -> 0%
where the time goes in v2:
time: 69.5 us; the launch traced here: 69.2 us
  Pallas kernels  69.2 us (100%)
    pallas_call x1, Pallas kernels, local(): pl.pallas_call(main_kernel, out_shape=(shape(LEAF, 64, PTS), shape(18, 64...  49.2 us
    pallas_call x1, Pallas kernels, local(): pl.pallas_call(rest_kernel, out_shape=shape(64, wide), in_specs=[SM] + [A...  18.2 us
    pallas_call x1, Pallas kernels, local(): pl.pallas_call(list_kernel, out_shape=shape(16, PTS, dtype=jnp.int32), in...  1.76 us

profile of v2, /device:TPU:0, one launch (start us, length us, event | category | flops | bytes accessed | tf_op | source)
XLA Modules:
  0.0 69.2 jit_solution(9398872629178948306)
XLA Ops:
  0.0 1.8 %lists.1.list_ref = s32[16,256]{1,0:T(8,128)} custom-call(s32[9,24]{1,0:T(8,128)} %bitcast.5, s32[1,24]{1,0:T(1,128)} %bitcast.9), custom_call_target="tpu_custom_call" | custom-call | flops 1000 | bytes 1000 | tf_op jit(solution)/shard_map/lists/pallas_call | solution.py:529
  1.8 49.2 %main.1 = (f32[24,64,256]{2,1,0:T(8,128)}, f32[18,64,128]{2,1,0:T(8,128)}, f32[18,64,128]{2,1,0:T(8,128)}, f32[64,6144]{1,0:T(8,128)}, f32[48,8,256]{2,1,0:T(8,1...) custom-call(s32[16,256]{1,0:T(8,128)} %lists.1.list_ref, s32[8,24]{1,0:T(8,128)} %bitcast.6, ...), custom_call_target="tpu_custom_call" | custom-call | flops 1000 | bytes 1000 | tf_op jit(solution)/shard_map/main/pallas_call | solution.py:534
  51.0 18.2 %rest.1 = f32[64,6144]{1,0:T(8,128)} custom-call(s32[16,256]{1,0:T(8,128)} %lists.1.list_ref, f32[18,64,128]{2,1,0:T(8,128)} %get-tuple-element.12.own_hbm, f32[18,64,128]{2,1,0:T(8,128)} %get-tuple-element.13.p2_hbm, f32[64,6144]{1,0:T(8,128)} %get-tuple-element.14.x2_hbm, f32[24,64,256]{2,1,0:T(8,128)} %get-tuple-element.15.acc_hbm, ...), custom_call_target="tpu_custom_call" | custom-call | flops 1000 | bytes 1000 | tf_op jit(solution)/shard_map/rest/pallas_call | solution.py:565

commit v3 on v2

--- a/solution.py
+++ b/solution.py
@@ -18,11 +18,12 @@
 FAR0 = 8
 FAR1 = 4
 FAR2 = 4
-UNROLL = 18
+UNROLL = 24
 SLOTS = 5
 REST_ROW = 8
 COUNT_ROW = 9
-CHUNK = 512
+AHEAD = 2048
+STEP = 4
 GROUPS = 16
 MESH = pl.DeviceIdType.MESH
 inv_four_pi = 1.0 / (4.0 * math.pi)
@@ -272,7 +273,7 @@
     acc_out, pack_out, p2_ref, x2_ref, centres_out, feats_out, xs_out,
     coords, x, x1, basis, t1, t2, c0, c1, c2, pack, p1, p2, acc, targets, centres, feats, xs,
     part, parts, y2_part, y2_parts, y1, q_low, q_high, m_low, m_high,
-    load_sem, part_send, part_recv, y2_send, y2_recv, pack_send, pack_recv, e_send, e_recv, n_send, n_recv, out_sem,
+    load_sem, part_send, part_recv, y2_send, y2_recv, swap_send, swap_recv, out_sem,
 ):
     group = lax.axis_index("grp")
     lane = lax.axis_index("lane")
@@ -329,23 +330,20 @@
             ),
         )
 
-    def chunk(i, src, dst, send, recv, device):
-        at = (slice(None), pl.ds(pl.multiple_of(i * CHUNK, CHUNK), CHUNK))
-        return pltpu.make_async_remote_copy(src.at[at], dst.at[at], send.at[i], recv.at[i], device, MESH)
-
-    def near_chunks(i):
-        return chunk(i, x, x2_ref, n_send, n_recv, beyond), chunk(i, x, x1, e_send, e_recv, partner)
-
+    def swap(src, dst, i, device):
+        return pltpu.make_async_remote_copy(src, dst, swap_send.at[i], swap_recv.at[i], device, MESH)
+
+    swaps = [
+        swap(x, x1, 0, partner),
+        swap(x.at[:, 0:AHEAD], x2_ref.at[:, 0:AHEAD], 1, beyond),
+        swap(pack, p1, 2, partner),
+        swap(pack, p2, 3, beyond),
+        swap(x.at[:, AHEAD:], x2_ref.at[:, AHEAD:], 4, beyond),
+    ]
     for d in range(1, GROUPS):
         part_copy(d)[0].start()
-    packs = [
-        pltpu.make_async_remote_copy(pack, p2, pack_send.at[0], pack_recv.at[0], beyond, MESH),
-        pltpu.make_async_remote_copy(pack, p1, pack_send.at[1], pack_recv.at[1], partner, MESH),
-    ]
-    for c in packs:
-        c.start()
-    for c in near_chunks(0):
-        c.start()
+    swaps[0].start()
+    swaps[1].start()
 
     eye = identity()
     for leaf in range(LEAF):
@@ -356,18 +354,13 @@
     feats[2 * LEAF] = feats[0]
     xs[2 * LEAF] = jnp.zeros((128, PTS), bf16)
 
-    def leaves(i):
-        ls = [2 * i + u for u in range(2) for s in range(SLOTS)]
-        js = [list_ref[s, 2 * i + u] for u in range(2) for s in range(SLOTS)]
-        pairs(ls, [jnp.where(j == LEAF, 2 * LEAF, j) for j in js], targets, centres, feats, xs, acc)
-
-    def step(i, _):
-        for c in near_chunks(i + 1):
-            c.start()
-        leaves(i)
+    def leaves(i, _):
+        at = [STEP * i + u for u in range(STEP) for s in range(SLOTS)]
+        js = [list_ref[s, STEP * i + u] for u in range(STEP) for s in range(SLOTS)]
+        pairs(at, [jnp.where(j == LEAF, 2 * LEAF, j) for j in js], targets, centres, feats, xs, acc)
         return 0
 
-    lax.fori_loop(0, 4, step, 0)
+    lax.fori_loop(0, 2, leaves, 0)
 
     for c in loads[11:]:
         c.wait()
@@ -380,10 +373,12 @@
     for d in range(1, LANES):
         y2_copy(d)[0].start()
 
-    lax.fori_loop(4, LEAF // 2 - 1, step, 0)
-    leaves(LEAF // 2 - 1)
-
-    for c in packs:
+    for c in swaps[2:]:
+        c.start()
+
+    lax.fori_loop(2, LEAF // STEP, leaves, 0)
+
+    for c in swaps[2:4]:
         c.wait()
     for b, p in enumerate((pack, p1, p2)):
         for t in range(LEAF // 2):
@@ -431,11 +426,7 @@
 
     lax.fori_loop(0, MID, down, 0)
 
-    def arrived(i, _):
-        chunk(i, x, x1, e_send, e_recv, partner).wait()
-        return 0
-
-    lax.fori_loop(0, LEAF // 2, arrived, 0)
+    swaps[0].wait()
     for leaf in range(LEAF):
         prepare(p1, x1, leaf, LEAF + leaf, eye, centres, feats, xs)
     outs = [
@@ -455,18 +446,15 @@
     for d in range(1, LANES):
         y2_copy(d)[0].wait_send()
 
-    def sent(i, _):
-        chunk(i, x, x2_ref, n_send, n_recv, beyond).wait()
-        return 0
-
-    lax.fori_loop(0, LEAF // 2, sent, 0)
+    swaps[1].wait()
+    swaps[4].wait()
     for c in outs:
         c.wait()
 
 
 def rest_kernel(
     list_ref, own_hbm, p2_hbm, x2_hbm, acc_hbm, centres_hbm, feats_hbm, xs_hbm, out_ref,
-    own, p2, targets, centres, feats, xs, acc, x, sem,
+    own, p2, targets, centres, feats, xs, acc, x, sem, out_sem,
 ):
     moves = [
         pltpu.make_async_copy(src, dst, sem.at[i])
@@ -480,13 +468,15 @@
             ]
         )
     ]
-    for c in moves:
+    for c in moves[:6]:
         c.start()
     targets[LEAF] = jnp.zeros((8, PTS), f32)
     acc[LEAF] = jnp.zeros((64, PTS), f32)
     eye = identity()
     for c in moves[:6]:
         c.wait()
+    for c in moves[6:]:
+        c.start()
     for leaf in range(LEAF):
         targets[leaf] = leaf_rows(own, leaf)
         prepare(p2, x, leaf, 2 * LEAF + leaf, eye, centres, feats, xs)
@@ -500,8 +490,14 @@
             [lax.shift_right_logical(w, 7) for w in words], [w & 127 for w in words], targets, centres, feats, xs, acc
         )
 
-    for leaf in range(LEAF):
-        out_ref[:, leaf * PTS:leaf * PTS + PTS] = acc[leaf]
+    outs = [
+        pltpu.make_async_copy(acc.at[leaf], out_ref.at[:, leaf * PTS:leaf * PTS + PTS], out_sem.at[leaf])
+        for leaf in range(LEAF)
+    ]
+    for c in outs:
+        c.start()
+    for c in outs:
+        c.wait()
 
 
 VM = pl.BlockSpec(memory_space=pltpu.VMEM)
@@ -552,8 +548,8 @@
             pltpu.VMEM((LANES, 32, 128), f32), pltpu.VMEM((MID, 64, 128), f32),
             pltpu.VMEM((3 * LEAF, 128, 128), bf16), pltpu.VMEM((3 * LEAF, 128, 128), bf16),
             pltpu.VMEM((3 * MID, 128, 128), bf16), pltpu.VMEM((3 * MID, 128, 128), bf16),
-            DMA((17,)), DMA((GROUPS,)), DMA((GROUPS,)), DMA((LANES,)), DMA((LANES,)), DMA((2,)), DMA((2,)),
-            DMA((LEAF // 2,)), DMA((LEAF // 2,)), DMA((LEAF // 2,)), DMA((LEAF // 2,)), DMA((8,)),
+            DMA((17,)), DMA((GROUPS,)), DMA((GROUPS,)), DMA((LANES,)), DMA((LANES,)), DMA((5,)), DMA((5,)),
+            DMA((8,)),
         ],
         compiler_params=params(56, collective_id=0, has_side_effects=True),
         cost_estimate=cost(1000),
@@ -566,12 +562,12 @@
         rest_kernel,
         out_shape=shape(64, wide),
         in_specs=[SM] + [ANY] * 7,
-        out_specs=VM,
+        out_specs=ANY,
         scratch_shapes=[
             pltpu.VMEM((18, 64, 128), f32), pltpu.VMEM((18, 64, 128), f32), pltpu.VMEM((LEAF + 1, 8, PTS), f32),
             pltpu.VMEM((3 * LEAF, 8, PTS), f32), pltpu.VMEM((3 * LEAF, PTS, 128), bf16),
             pltpu.VMEM((3 * LEAF, 128, PTS), bf16), pltpu.VMEM((LEAF + 1, 64, PTS), f32), pltpu.VMEM((64, wide), f32),
-            DMA((12,)),
+            DMA((12,)), DMA((LEAF,)),
         ],
         compiler_params=params(56),
         cost_estimate=cost(1000),

time: 69.5 us -> 69.3 us (level)
  no operation moved by 1% of the time
where the time goes in v3:
time: 69.3 us; the launch traced here: 69 us
  Pallas kernels  69 us (100%)
    pallas_call x1, Pallas kernels, local(): pl.pallas_call(main_kernel, out_shape=(shape(LEAF, 64, PTS), shape(18, 64...  48.8 us
    pallas_call x1, Pallas kernels, local(): pl.pallas_call(rest_kernel, out_shape=shape(64, wide), in_specs=[SM] + [A...  18.5 us
    pallas_call x1, Pallas kernels, local(): pl.pallas_call(list_kernel, out_shape=shape(16, PTS, dtype=jnp.int32), in...  1.76 us

profile of v3, /device:TPU:0, one launch (start us, length us, event | category | flops | bytes accessed | tf_op | source)
XLA Modules:
  0.0 69.0 jit_solution(13910107442163360055)
XLA Ops:
  0.0 1.8 %lists.1.list_ref = s32[16,256]{1,0:T(8,128)} custom-call(s32[9,24]{1,0:T(8,128)} %bitcast.5, s32[1,24]{1,0:T(1,128)} %bitcast.9), custom_call_target="tpu_custom_call" | custom-call | flops 1000 | bytes 1000 | tf_op jit(solution)/shard_map/lists/pallas_call | solution.py:525
  1.8 48.8 %main.1 = (f32[24,64,256]{2,1,0:T(8,128)}, f32[18,64,128]{2,1,0:T(8,128)}, f32[18,64,128]{2,1,0:T(8,128)}, f32[64,6144]{1,0:T(8,128)}, f32[48,8,256]{2,1,0:T(8,1...) custom-call(s32[16,256]{1,0:T(8,128)} %lists.1.list_ref, s32[8,24]{1,0:T(8,128)} %bitcast.6, ...), custom_call_target="tpu_custom_call" | custom-call | flops 1000 | bytes 1000 | tf_op jit(solution)/shard_map/main/pallas_call | solution.py:530
  50.5 18.5 %rest.1 = f32[64,6144]{1,0:T(8,128)} custom-call(s32[16,256]{1,0:T(8,128)} %lists.1.list_ref, f32[18,64,128]{2,1,0:T(8,128)} %get-tuple-element.12.own_hbm, f32[18,64,128]{2,1,0:T(8,128)} %get-tuple-element.13.p2_hbm, f32[64,6144]{1,0:T(8,128)} %get-tuple-element.14.x2_hbm, f32[24,64,256]{2,1,0:T(8,128)} %get-tuple-element.15.acc_hbm, ...), custom_call_target="tpu_custom_call" | custom-call | flops 1000 | bytes 1000 | tf_op jit(solution)/shard_map/rest/pallas_call | solution.py:561

commit v4 on v3

--- a/solution.py
+++ b/solution.py
@@ -22,7 +22,6 @@
 SLOTS = 5
 REST_ROW = 8
 COUNT_ROW = 9
-AHEAD = 2048
 STEP = 4
 GROUPS = 16
 MESH = pl.DeviceIdType.MESH
@@ -334,16 +333,15 @@
         return pltpu.make_async_remote_copy(src, dst, swap_send.at[i], swap_recv.at[i], device, MESH)
 
     swaps = [
-        swap(x, x1, 0, partner),
-        swap(x.at[:, 0:AHEAD], x2_ref.at[:, 0:AHEAD], 1, beyond),
-        swap(pack, p1, 2, partner),
-        swap(pack, p2, 3, beyond),
-        swap(x.at[:, AHEAD:], x2_ref.at[:, AHEAD:], 4, beyond),
+        swap(pack, p2, 0, beyond),
+        swap(pack, p1, 1, partner),
+        swap(x, x1, 2, partner),
+        swap(x, x2_ref, 3, beyond),
     ]
     for d in range(1, GROUPS):
         part_copy(d)[0].start()
-    swaps[0].start()
-    swaps[1].start()
+    for c in swaps[:3]:
+        c.start()
 
     eye = identity()
     for leaf in range(LEAF):
@@ -373,20 +371,21 @@
     for d in range(1, LANES):
         y2_copy(d)[0].start()
 
-    for c in swaps[2:]:
-        c.start()
-
-    lax.fori_loop(2, LEAF // STEP, leaves, 0)
-
-    for c in swaps[2:4]:
-        c.wait()
+    lax.fori_loop(2, 4, leaves, 0)
+
+    for c in swaps[:2]:
+        c.wait()
+    for d in range(1, LANES):
+        y2_copy(d)[1].wait_recv()
+    swaps[3].start()
+
+    lax.fori_loop(4, LEAF // STEP, leaves, 0)
+
     for b, p in enumerate((pack, p1, p2)):
         for t in range(LEAF // 2):
             place_tile(p[t], q_low, q_high, LEAF * b + 2 * t)
         for t in range(MID // 2):
             place_tile(p[LEAF // 2 + t], m_low, m_high, MID * b + 2 * t)
-    for d in range(1, LANES):
-        y2_copy(d)[1].wait_recv()
     y2 = y2_parts[0]
     for r in range(1, LANES):
         y2 = y2 + y2_parts[r]
@@ -426,7 +425,7 @@
 
     lax.fori_loop(0, MID, down, 0)
 
-    swaps[0].wait()
+    swaps[2].wait()
     for leaf in range(LEAF):
         prepare(p1, x1, leaf, LEAF + leaf, eye, centres, feats, xs)
     outs = [
@@ -446,8 +445,7 @@
     for d in range(1, LANES):
         y2_copy(d)[0].wait_send()
 
-    swaps[1].wait()
-    swaps[4].wait()
+    swaps[3].wait()
     for c in outs:
         c.wait()
 
@@ -548,7 +546,7 @@
             pltpu.VMEM((LANES, 32, 128), f32), pltpu.VMEM((MID, 64, 128), f32),
             pltpu.VMEM((3 * LEAF, 128, 128), bf16), pltpu.VMEM((3 * LEAF, 128, 128), bf16),
             pltpu.VMEM((3 * MID, 128, 128), bf16), pltpu.VMEM((3 * MID, 128, 128), bf16),
-            DMA((17,)), DMA((GROUPS,)), DMA((GROUPS,)), DMA((LANES,)), DMA((LANES,)), DMA((5,)), DMA((5,)),
+            DMA((17,)), DMA((GROUPS,)), DMA((GROUPS,)), DMA((LANES,)), DMA((LANES,)), DMA((4,)), DMA((4,)),
             DMA((8,)),
         ],
         compiler_params=params(56, collective_id=0, has_side_effects=True),

time: 69.3 us -> 65.5 us (0.945)
  Pallas kernels: 69 us -> 65 us
    pallas_call x1, Pallas kernels: 48.8 us -> 44.7 us  [local(): pl.pallas_call(main_kernel, out_shape=(shape(LEAF, 64, PTS), shape(18, 64...]
where the time goes in v4:
time: 65.5 us; the launch traced here: 65.2 us
  Pallas kernels  65 us (99%)
    pallas_call x1, Pallas kernels, local(): pl.pallas_call(main_kernel, out_shape=(shape(LEAF, 64, PTS), shape(18, 64...  44.7 us
    pallas_call x1, Pallas kernels, local(): pl.pallas_call(rest_kernel, out_shape=shape(64, wide), in_specs=[SM] + [A...  18.5 us
    pallas_call x1, Pallas kernels, local(): pl.pallas_call(list_kernel, out_shape=shape(16, PTS, dtype=jnp.int32), in...  1.76 us

profile of v4, /device:TPU:0, one launch (start us, length us, event | category | flops | bytes accessed | tf_op | source)
XLA Modules:
  0.0 65.2 jit_solution(11163514141848407702)
XLA Ops:
  0.0 1.8 %lists.1.list_ref = s32[16,256]{1,0:T(8,128)} custom-call(s32[9,24]{1,0:T(8,128)} %bitcast.5, s32[1,24]{1,0:T(1,128)} %bitcast.9), custom_call_target="tpu_custom_call" | custom-call | flops 1000 | bytes 1000 | tf_op jit(solution)/shard_map/lists/pallas_call | solution.py:523
  1.8 44.7 %main.1 = (f32[24,64,256]{2,1,0:T(8,128)}, f32[18,64,128]{2,1,0:T(8,128)}, f32[18,64,128]{2,1,0:T(8,128)}, f32[64,6144]{1,0:T(8,128)}, f32[48,8,256]{2,1,0:T(8,1...) custom-call(s32[16,256]{1,0:T(8,128)} %lists.1.list_ref, s32[8,24]{1,0:T(8,128)} %bitcast.6, ...), custom_call_target="tpu_custom_call" | custom-call | flops 1000 | bytes 1000 | tf_op jit(solution)/shard_map/main/pallas_call | solution.py:528
  46.5 18.5 %rest.1 = f32[64,6144]{1,0:T(8,128)} custom-call(s32[16,256]{1,0:T(8,128)} %lists.1.list_ref, f32[18,64,128]{2,1,0:T(8,128)} %get-tuple-element.12.own_hbm, f32[18,64,128]{2,1,0:T(8,128)} %get-tuple-element.13.p2_hbm, f32[64,6144]{1,0:T(8,128)} %get-tuple-element.14.x2_hbm, f32[24,64,256]{2,1,0:T(8,128)} %get-tuple-element.15.acc_hbm, ...), custom_call_target="tpu_custom_call" | custom-call | flops 1000 | bytes 1000 | tf_op jit(solution)/shard_map/rest/pallas_call | solution.py:559

commit v5 on v4

--- a/solution.py
+++ b/solution.py
@@ -271,7 +271,7 @@
     list_ref, far0_ref, far1_ref, far2_ref, coords_hbm, x_hbm, basis_hbm, t1_hbm, t2_hbm, c0_hbm, c1_hbm, c2_hbm,
     acc_out, pack_out, p2_ref, x2_ref, centres_out, feats_out, xs_out,
     coords, x, x1, basis, t1, t2, c0, c1, c2, pack, p1, p2, acc, targets, centres, feats, xs,
-    part, parts, y2_part, y2_parts, y1, q_low, q_high, m_low, m_high,
+    part, parts, y2_part, y2_parts, y1, y1_part, y0, q_low, q_high, m_low, m_high,
     load_sem, part_send, part_recv, y2_send, y2_recv, swap_send, swap_recv, out_sem,
 ):
     group = lax.axis_index("grp")
@@ -340,7 +340,7 @@
     ]
     for d in range(1, GROUPS):
         part_copy(d)[0].start()
-    for c in swaps[:3]:
+    for c in swaps:
         c.start()
 
     eye = identity()
@@ -371,59 +371,33 @@
     for d in range(1, LANES):
         y2_copy(d)[0].start()
 
-    lax.fori_loop(2, 4, leaves, 0)
+    lax.fori_loop(2, LEAF // STEP, leaves, 0)
 
     for c in swaps[:2]:
         c.wait()
-    for d in range(1, LANES):
-        y2_copy(d)[1].wait_recv()
-    swaps[3].start()
-
-    lax.fori_loop(4, LEAF // STEP, leaves, 0)
-
     for b, p in enumerate((pack, p1, p2)):
         for t in range(LEAF // 2):
             place_tile(p[t], q_low, q_high, LEAF * b + 2 * t)
         for t in range(MID // 2):
             place_tile(p[LEAF // 2 + t], m_low, m_high, MID * b + 2 * t)
-    y2 = y2_parts[0]
-    for r in range(1, LANES):
-        y2 = y2 + y2_parts[r]
-    other = swap_halves(y2)
-    low = lanes_low(y2.shape)
-    y2 = jnp.concatenate([jnp.where(low, y2, other), jnp.where(low, other, y2)], axis=0)
-
     for t in range(MID // 2):
         at = slice(t * 128, t * 128 + 128)
-        y = coupled(
+        y1_part[t] = coupled(
             [[source_of(far1_ref[f, 2 * t + i], place, MID) for f in range(FAR1)] for i in range(2)],
             [c1[f, :, at] for f in range(FAR1)], m_low, m_high,
         )
-        w = t2[:, at]
-        one, two = transposed(*halves(y2), jnp.concatenate([w, w], axis=0))
-        y = y + jnp.where(lanes_low(y.shape), one, two)
-        other = swap_halves(y)
-        low = lanes_low(y.shape)
-        y1[2 * t] = jnp.where(low, y, other)
-        y1[2 * t + 1] = jnp.where(low, other, y)
-
-    def down(m, _):
+
+    def across(m, _):
         for u in range(2):
             t = 2 * m + u
             at = pl.ds(pl.multiple_of(t * 128, 128), 128)
-            y = coupled(
+            y0[t] = coupled(
                 [[source_of(far0_ref[f, 2 * t + i], place, LEAF) for f in range(FAR0)] for i in range(2)],
                 [c0[f, :, at] for f in range(FAR0)], q_low, q_high,
             )
-            w = t1[:, at]
-            one, two = transposed(*halves(y1[m]), jnp.concatenate([w, w], axis=0))
-            y = y + jnp.where(lanes_low(y.shape), one, two)
-            one, two = transposed(*halves(y), basis[:, at])
-            acc[2 * t] += one
-            acc[2 * t + 1] += two
         return 0
 
-    lax.fori_loop(0, MID, down, 0)
+    lax.fori_loop(0, MID, across, 0)
 
     swaps[2].wait()
     for leaf in range(LEAF):
@@ -432,14 +406,44 @@
         pltpu.make_async_copy(src, dst, out_sem.at[i])
         for i, (src, dst) in enumerate(
             [
-                (acc, acc_out), (pack, pack_out), (p2, p2_ref), (centres.at[0:48], centres_out),
+                (pack, pack_out), (p2, p2_ref), (centres.at[0:48], centres_out),
                 (feats.at[0:24], feats_out.at[0:24]), (feats.at[24:48], feats_out.at[24:48]),
                 (xs.at[0:24], xs_out.at[0:24]), (xs.at[24:48], xs_out.at[24:48]),
+                (acc, acc_out),
             ]
         )
     ]
-    for c in outs:
+    for c in outs[:-1]:
         c.start()
+
+    for d in range(1, LANES):
+        y2_copy(d)[1].wait_recv()
+    y2 = y2_parts[0]
+    for r in range(1, LANES):
+        y2 = y2 + y2_parts[r]
+    other = swap_halves(y2)
+    low = lanes_low(y2.shape)
+    y2 = jnp.concatenate([jnp.where(low, y2, other), jnp.where(low, other, y2)], axis=0)
+    for t in range(MID // 2):
+        w = t2[:, t * 128:t * 128 + 128]
+        one, two = transposed(*halves(y2), jnp.concatenate([w, w], axis=0))
+        y = y1_part[t] + jnp.where(lanes_low(one.shape), one, two)
+        other = swap_halves(y)
+        low = lanes_low(y.shape)
+        y1[2 * t] = jnp.where(low, y, other)
+        y1[2 * t + 1] = jnp.where(low, other, y)
+
+    for m in range(MID):
+        for u in range(2):
+            t = 2 * m + u
+            at = slice(t * 128, t * 128 + 128)
+            w = t1[:, at]
+            one, two = transposed(*halves(y1[m]), jnp.concatenate([w, w], axis=0))
+            y = y0[t] + jnp.where(lanes_low(one.shape), one, two)
+            one, two = transposed(*halves(y), basis[:, at])
+            acc[2 * t] += one
+            acc[2 * t + 1] += two
+    outs[-1].start()
     for d in range(1, GROUPS):
         part_copy(d)[0].wait_send()
     for d in range(1, LANES):
@@ -466,15 +470,13 @@
             ]
         )
     ]
-    for c in moves[:6]:
+    for c in moves:
         c.start()
     targets[LEAF] = jnp.zeros((8, PTS), f32)
     acc[LEAF] = jnp.zeros((64, PTS), f32)
     eye = identity()
     for c in moves[:6]:
         c.wait()
-    for c in moves[6:]:
-        c.start()
     for leaf in range(LEAF):
         targets[leaf] = leaf_rows(own, leaf)
         prepare(p2, x, leaf, 2 * LEAF + leaf, eye, centres, feats, xs)
@@ -544,6 +546,7 @@
             pltpu.VMEM((2 * LEAF + 1, 128, PTS), bf16),
             pltpu.VMEM((32, 128), f32), pltpu.VMEM((GROUPS, 32, 128), f32), pltpu.VMEM((32, 128), f32),
             pltpu.VMEM((LANES, 32, 128), f32), pltpu.VMEM((MID, 64, 128), f32),
+            pltpu.VMEM((MID // 2, 64, 128), f32), pltpu.VMEM((LEAF // 2, 64, 128), f32),
             pltpu.VMEM((3 * LEAF, 128, 128), bf16), pltpu.VMEM((3 * LEAF, 128, 128), bf16),
             pltpu.VMEM((3 * MID, 128, 128), bf16), pltpu.VMEM((3 * MID, 128, 128), bf16),
             DMA((17,)), DMA((GROUPS,)), DMA((GROUPS,)), DMA((LANES,)), DMA((LANES,)), DMA((4,)), DMA((4,)),

time: 65.5 us -> 63.9 us (0.976)
  the two profiles are of different devices: /device:TPU:0 before, /device:TPU:1 now
where the time goes in v5:
time: 63.9 us; the launch traced here: 63.6 us
  Pallas kernels  63.6 us (100%)
    pallas_call x1, Pallas kernels, local(): pl.pallas_call(main_kernel, out_shape=(shape(LEAF, 64, PTS), shape(18, 64...  44.3 us
    pallas_call x1, Pallas kernels, local(): pl.pallas_call(rest_kernel, out_shape=shape(64, wide), in_specs=[SM] + [A...  17.5 us
    pallas_call x1, Pallas kernels, local(): pl.pallas_call(list_kernel, out_shape=shape(16, PTS, dtype=jnp.int32), in...  1.76 us

profile of v5, /device:TPU:1, one launch (start us, length us, event | category | flops | bytes accessed | tf_op | source)
XLA Modules:
  0.0 63.6 jit_solution(18040107634818801135)
XLA Ops:
  0.0 1.8 %lists.1.list_ref = s32[16,256]{1,0:T(8,128)} custom-call(s32[9,24]{1,0:T(8,128)} %bitcast.5, s32[1,24]{1,0:T(1,128)} %bitcast.9), custom_call_target="tpu_custom_call" | custom-call | flops 1000 | bytes 1000 | tf_op jit(solution)/shard_map/lists/pallas_call | solution.py:525
  1.8 44.3 %main.1 = (f32[24,64,256]{2,1,0:T(8,128)}, f32[18,64,128]{2,1,0:T(8,128)}, f32[18,64,128]{2,1,0:T(8,128)}, f32[64,6144]{1,0:T(8,128)}, f32[48,8,256]{2,1,0:T(8,1...) custom-call(s32[16,256]{1,0:T(8,128)} %lists.1.list_ref, s32[8,24]{1,0:T(8,128)} %bitcast.6, ...), custom_call_target="tpu_custom_call" | custom-call | flops 1000 | bytes 1000 | tf_op jit(solution)/shard_map/main/pallas_call | solution.py:530
  46.1 17.5 %rest.1 = f32[64,6144]{1,0:T(8,128)} custom-call(s32[16,256]{1,0:T(8,128)} %lists.1.list_ref, f32[18,64,128]{2,1,0:T(8,128)} %get-tuple-element.12.own_hbm, f32[18,64,128]{2,1,0:T(8,128)} %get-tuple-element.13.p2_hbm, f32[64,6144]{1,0:T(8,128)} %get-tuple-element.14.x2_hbm, f32[24,64,256]{2,1,0:T(8,128)} %get-tuple-element.15.acc_hbm, ...), custom_call_target="tpu_custom_call" | custom-call | flops 1000 | bytes 1000 | tf_op jit(solution)/shard_map/rest/pallas_call | solution.py:562

commit v6 on v5

--- a/solution.py
+++ b/solution.py
@@ -22,7 +22,7 @@
 SLOTS = 5
 REST_ROW = 8
 COUNT_ROW = 9
-STEP = 4
+STEP = 6
 GROUPS = 16
 MESH = pl.DeviceIdType.MESH
 inv_four_pi = 1.0 / (4.0 * math.pi)
@@ -358,7 +358,7 @@
         pairs(at, [jnp.where(j == LEAF, 2 * LEAF, j) for j in js], targets, centres, feats, xs, acc)
         return 0
 
-    lax.fori_loop(0, 2, leaves, 0)
+    lax.fori_loop(0, 1, leaves, 0)
 
     for c in loads[11:]:
         c.wait()
@@ -371,7 +371,7 @@
     for d in range(1, LANES):
         y2_copy(d)[0].start()
 
-    lax.fori_loop(2, LEAF // STEP, leaves, 0)
+    lax.fori_loop(1, LEAF // STEP, leaves, 0)
 
     for c in swaps[:2]:
         c.wait()

time: 63.9 us -> 63.3 us (level)
  the two profiles are of different devices: /device:TPU:1 before, /device:TPU:0 now
where the time goes in v6:
time: 63.3 us; the launch traced here: 62.4 us
  Pallas kernels  62.2 us (98%)
    pallas_call x1, Pallas kernels, local(): pl.pallas_call(main_kernel, out_shape=(shape(LEAF, 64, PTS), shape(18, 64...  42.9 us
    pallas_call x1, Pallas kernels, local(): pl.pallas_call(rest_kernel, out_shape=shape(64, wide), in_specs=[SM] + [A...  17.5 us
    pallas_call x1, Pallas kernels, local(): pl.pallas_call(list_kernel, out_shape=shape(16, PTS, dtype=jnp.int32), in...  1.76 us

profile of v6, /device:TPU:0, one launch (start us, length us, event | category | flops | bytes accessed | tf_op | source)
XLA Modules:
  0.0 62.4 jit_solution(6636311569592366375)
XLA Ops:
  0.0 1.8 %lists.1.list_ref = s32[16,256]{1,0:T(8,128)} custom-call(s32[9,24]{1,0:T(8,128)} %bitcast.5, s32[1,24]{1,0:T(1,128)} %bitcast.9), custom_call_target="tpu_custom_call" | custom-call | flops 1000 | bytes 1000 | tf_op jit(solution)/shard_map/lists/pallas_call | solution.py:525
  1.8 42.9 %main.1 = (f32[24,64,256]{2,1,0:T(8,128)}, f32[18,64,128]{2,1,0:T(8,128)}, f32[18,64,128]{2,1,0:T(8,128)}, f32[64,6144]{1,0:T(8,128)}, f32[48,8,256]{2,1,0:T(8,1...) custom-call(s32[16,256]{1,0:T(8,128)} %lists.1.list_ref, s32[8,24]{1,0:T(8,128)} %bitcast.6, ...), custom_call_target="tpu_custom_call" | custom-call | flops 1000 | bytes 1000 | tf_op jit(solution)/shard_map/main/pallas_call | solution.py:530
  44.7 17.5 %rest.1 = f32[64,6144]{1,0:T(8,128)} custom-call(s32[16,256]{1,0:T(8,128)} %lists.1.list_ref, f32[18,64,128]{2,1,0:T(8,128)} %get-tuple-element.12.own_hbm, f32[18,64,128]{2,1,0:T(8,128)} %get-tuple-element.13.p2_hbm, f32[64,6144]{1,0:T(8,128)} %get-tuple-element.14.x2_hbm, f32[24,64,256]{2,1,0:T(8,128)} %get-tuple-element.15.acc_hbm, ...), custom_call_target="tpu_custom_call" | custom-call | flops 1000 | bytes 1000 | tf_op jit(solution)/shard_map/rest/pallas_call | solution.py:562
